TPU v7x, 256 devices: a whole 4x4x8 slice. The times are simulated.
256 devices in a mesh: ma: 128 (over z, y, x), bl: 2 (over core).
Axes of the slice: x: 4, y: 4, z: 8, core: 2. Of those that a mesh axis runs over, the one named last changes fastest.
Arguments:
- vis: float32 [2, 4096, 2048], P(None, 'ma', 'bl'), may hold values from -6 to 6
- counts: int32 [2048], P('bl'), may hold values from 1 to 256
- m_order: int32 [512], replicated, may hold values from 0 to 511, as said below
- beam: bfloat16 [512, 2, 2048, 512], P('ma', None, 'bl'), may hold values from -0.125 to 0.125
- row_counts: int32 [128], replicated, may hold values from 1 to 8, 512 in all
Outputs:
- alm_grad: float32 [2, 128, 4, 1024], P(None, None, 'bl', 'ma')
Inputs may be any that keep to these rules, and one draw needn't show every extreme that they name: `m_order`: slot values are distinct multiples of 1 minus one, plus 512 // 512; every such value in range appears once. `row_counts`: counts sum to 512; each is at least 1 and one of them is exactly 8.
All inputs are finite; a program needn't handle non-finite values.
Results may differ from a plain program's by a relative error of at most 0.0029.
Values sent between devices are 32-bit elements; how exact they have to be, the bound alone decides.
No kernel may reach another device: no remote copies, remote signals or barrier semaphores. Data moves between devices by JAX's collectives and lax.ppermute only.
A program may use at most 64 MiB of HBM per device.

v0:
```python
import jax
import jax.numpy as jnp
from jax import lax
from jax.sharding import PartitionSpec as P

L = 512


def transform_tables(m_values, times, total_times):
    turns = m_values[:, None] * times[None, :] % total_times
    phase = 2.0 * jnp.pi / total_times * turns.astype(jnp.float32)
    norm = 1.0 / jnp.sqrt(jnp.float32(total_times))
    return (jnp.cos(phase) * norm, jnp.sin(phase) * norm)


def sidereal(cosine, sine, vis_re, vis_im):
    high = lax.Precision.HIGHEST
    modes_re = jnp.dot(cosine, vis_re, precision=high) + jnp.dot(sine, vis_im, precision=high)
    modes_im = jnp.dot(cosine, vis_im, precision=high) - jnp.dot(sine, vis_re, precision=high)
    return jnp.stack([modes_re, modes_im], axis=1)


def body(vis, counts, m_order, beam, row_counts):
    shards = lax.axis_size("ma")
    position = lax.axis_index("ma")
    time_dev = vis.shape[1]
    slots_dev = beam.shape[0]
    total_times = time_dev * shards
    own_times = position * time_dev + jnp.arange(time_dev, dtype=jnp.int32)
    cosine, sine = transform_tables(m_order, own_times, total_times)
    modes = lax.psum_scatter(
        sidereal(cosine, sine, vis[0], vis[1]), "ma", scatter_dimension=0, tiled=True
    )
    scale = counts.astype(jnp.float32) / 256.0
    weighted = (modes * scale[None, None, :]).astype(jnp.bfloat16)
    beam_re = beam[:, 0]
    beam_im = beam[:, 1]
    w_re = weighted[:, 0]
    w_im = weighted[:, 1]
    form = "kb,kbl->kl"
    out_re = jnp.einsum(form, w_re, beam_re, preferred_element_type=jnp.float32) + jnp.einsum(
        form, w_im, beam_im, preferred_element_type=jnp.float32
    )
    out_im = jnp.einsum(form, w_im, beam_re, preferred_element_type=jnp.float32) - jnp.einsum(
        form, w_re, beam_im, preferred_element_type=jnp.float32
    )
    ells = jnp.arange(L, dtype=jnp.int32)
    my_m = lax.dynamic_slice_in_dim(m_order, position * slots_dev, slots_dev, 0)
    keep = ells[None, :] >= my_m[:, None]
    partial_alm = jnp.stack([jnp.where(keep, out_re, 0.0), jnp.where(keep, out_im, 0.0)], axis=1)
    half_slots = slots_dev // lax.axis_size("bl")
    summed = lax.psum(partial_alm, "bl")
    mine = lax.dynamic_slice_in_dim(summed, lax.axis_index("bl") * half_slots, half_slots, 0)
    rowcap = 2 * L // shards
    starts = jnp.cumsum(row_counts) - row_counts
    within = jnp.arange(rowcap, dtype=jnp.int32)
    ell_index = jnp.clip(starts[:, None] + within[None, :], 0, L - 1)
    valid = within[None, :] < row_counts[:, None]
    picked = jnp.take(mine, ell_index.reshape(-1), axis=2).reshape(half_slots, 2, shards, rowcap)
    picked = jnp.where(valid[None, None, :, :], picked, 0.0)
    outgoing = jnp.transpose(picked, (1, 2, 0, 3))
    return lax.all_to_all(outgoing, "ma", split_axis=1, concat_axis=1, tiled=True)


def solution(mesh):
    placed = (P(None, "ma", "bl"), P("bl"), P(), P("ma", None, "bl", None), P())
    return jax.shard_map(
        body, mesh=mesh, in_specs=placed, out_specs=P(None, None, "bl", "ma"), check_vma=False
    )
```

profile of v0, /device:TPU:1, one launch (start us, length us, event | category | flops | bytes accessed | tf_op | source)
XLA Modules:
  0.0 316.3 jit_solution(3992565695133505316)
XLA Ops:
  6.5 3.7 %fusion.16 = f32[512,1024]{1,0:T(8,128)S(1)} fusion(s32[32]{0:T(128)S(1)} %iota_add_fusion, s32[512]{0:T(512)} %param.7, f32[2,32,1024]{2,1,0:T(8,128)} %param.5), kind=kOutput, calls=%fused_computation.28 | convolution fusion | flops 201572352 | bytes 2230400 | tf_op jit(solution)/shard_map/dot_general | solution.py:18
  10.2 3.6 %fusion.15 = f32[512,1024]{1,0:T(8,128)S(1)} fusion(s32[32]{0:T(128)S(1)} %iota_add_fusion, s32[512]{0:T(512)} %param.7, f32[2,32,1024]{2,1,0:T(8,128)} %param.5), kind=kOutput, calls=%fused_computation.27 | convolution fusion | flops 201572352 | bytes 2230400 | tf_op jit(solution)/shard_map/dot_general | solution.py:19
  13.9 2.8 add_bitcast_fusion
  16.7 2.8 subtract_bitcast_fusion
  19.5 2.3 pad_maximum_fusion
  21.9 0.5 copy-done.3
  22.4 0.1 copy.21
  22.5 0.2 reduce-window.9
  23.0 0.6 dynamic-slice
  24.3 0.1 iota_compare_fusion
  24.4 232.3 %all-reduce.3.cloned.1.call-done = f32[512,2,1024]{2,0,1:T(8,128)} async-done(((f32[512,2,1024]{2,0,1:T(8,128)}), f32[512,2,1024]{2,0,1:T(8,128)}) %all-reduce.3.cloned.1.call-update) | async-done | bytes 4194320
  256.7 0.9 fusion.33
  257.6 2.8 fusion.2
  260.5 2.8 fusion.4
  263.3 2.8 fusion
  266.1 2.8 fusion.6
  269.1 0.4 copy.22
  269.5 10.5 %psum.7 = f32[4,2,512]{1,0,2:T(4,128)S(1)} all-reduce(f32[4,2,512]{1,0,2:T(4,128)S(1)} %copy.22), channel_id=1, replica_groups=mesh['ma'=128,'bl'=2] {'bl'}, use_global_device_ids=true, to_apply=%region_2.3 | all-reduce | flops 4096 | bytes 32768 | tf_op jit(solution)/shard_map/psum | solution.py:52
  280.0 0.2 constant_dynamic-slice_fusion
  280.3 3.6 %gather_fusion = f32[1024,2,2]{2,1,0:T(2,128)S(1)} fusion(f32[2,2,512]{1,0,2:T(2,128)S(1)} %constant_dynamic-slice_fusion, s32[1024]{0:T(1024)S(1)} %broadcast_clamp_fusion), kind=kCustom, calls=%fused_computation | custom fusion | bytes 36864 | tf_op jit(solution)/shard_map/jit(_take)/gather | solution.py:59
  283.8 1.9 copy.32
  285.8 0.2 copy.24
  286.0 22.8 %all_to_all.5 = f32[2,128,2,8]{3,0,2,1:T(2,128)S(1)} all-to-all(f32[2,128,2,8]{3,0,2,1:T(2,128)S(1)} %copy.24), channel_id=1, replica_groups=mesh['ma'=128,'bl'=2] {'ma'}, dimensions={1} | all-to-all | bytes 32768 | tf_op jit(solution)/shard_map/all_to_all | solution.py:62
  308.8 0.7 copy.25
  (24 shorter events, 0.6 us)
Async XLA Ops:
  6.5 7.3 %copy-start = (f32[2,32,1024]{2,1,0:T(8,128)S(1)}, f32[2,32,1024]{2,1,0:T(8,128)}, u32[]{:S(2)}) copy-start(f32[2,32,1024]{2,1,0:T(8,128)} %param.5) | copy-start | bytes 786436
  6.5 7.3 %copy-start.1 = (s32[512]{0:T(512)S(1)}, s32[512]{0:T(512)}, u32[]{:S(2)}) copy-start(s32[512]{0:T(512)} %param.7) | copy-start | bytes 6148
  6.5 250.2 %all-reduce.3.cloned.1.call-start = ((), (), s32[]{:S(2)}) async-start(), calls=%async_computation.1 | async-start | bytes 8388608
  21.7 0.7 copy-start.3
  21.7 1.3 copy-start.4
  21.8 2.5 copy-start.2
Sparse Core Ops, SparseCore 0:
  21.9 234.8 all-reduce.2
where the time goes:
time: 317 us; the launch traced here: 316 us
  waiting for transfers between devices  232 us (73%)
  blocking collectives  33.3 us (11%)
  matrix products  24.2 us (8%)
  between operations  14.3 us (5%)
  local copies, waits for them, and re-layouts  8.42 us (3%)
  other arithmetic  3.75 us (1%)
    unnamed x2, waiting for transfers between devices  232 us
    all_to_all x1, blocking collectives, body(): lax.all_to_all(outgoing, 'ma', split_axis=1, concat_axis=1, tiled=True)  22.8 us
    psum x1, blocking collectives, body(): summed = lax.psum(partial_alm, 'bl')  10.5 us
  transfers between devices with their start and end apart: 1, of which 1 were waited for; matrix products, arithmetic and copies ran while one was open for 0% of the time, Pallas kernels for 0%

commit v1 on v0

v1 whole, which is shorter than its diff:
```python
import numpy as np
import jax
import jax.numpy as jnp
from jax import lax
from jax.experimental import pallas as pl
from jax.experimental.pallas import tpu as pltpu
from jax.sharding import Mesh
from jax.sharding import PartitionSpec as P

L = 512
TIMES = 4096
OUTER = 8
INNER = 16
SPAN = TIMES // OUTER
OWNERS = OUTER * INNER
SLOTS = 4
ROWCAP = 8
LANES = 128
HALF = 64

F32 = jnp.float32
BF16 = jnp.bfloat16
VMEM = pl.BlockSpec(memory_space=pltpu.VMEM)
SMEM = pl.BlockSpec(memory_space=pltpu.SMEM)
ANY = pl.BlockSpec(memory_space=pl.ANY)


def transform_tables():
    turns = np.outer(np.arange(L), np.arange(SPAN)) % TIMES
    phase = 2.0 * np.pi / TIMES * turns
    table = np.concatenate([np.cos(phase), np.sin(phase)], axis=1) / np.sqrt(TIMES)
    table = table.astype(np.float32)
    high = table.astype(BF16)
    low = (table - high.astype(np.float32)).astype(BF16)
    return high, low


def low_lanes(shape):
    return lax.broadcasted_iota(jnp.int32, shape, 1) < HALF


def quarter_turn(pair):
    turned = pltpu.roll(pair, HALF, 1)
    return jnp.where(low_lanes(pair.shape), turned, -turned)


def split(array):
    high = array.astype(BF16)
    return high, (array - high.astype(F32)).astype(BF16)


def pack_kernel(vis_ref, counts_ref, out_ref):
    low = low_lanes((vis_ref.shape[1], LANES))
    for j in range(vis_ref.shape[2] // LANES):
        lanes = slice(j * LANES, (j + 1) * LANES)
        scale = counts_ref[j : j + 1, :].astype(F32) * (1.0 / 256.0)
        re = vis_ref[0, :, lanes] * scale
        im = vis_ref[1, :, lanes] * scale
        out_ref[2 * j] = jnp.where(low, re, pltpu.roll(im, HALF, 1))
        out_ref[2 * j + 1] = jnp.where(low, pltpu.roll(re, HALF, 1), im)


def transform_kernel(order_ref, place_ref, x_ref, high_ref, low_ref, out_ref, modes_ref):
    x = x_ref[...]
    high, low = split(jnp.concatenate([x, quarter_turn(x)], axis=0))
    wide = jnp.dot(
        high_ref[...], jnp.concatenate([high, low], axis=1), preferred_element_type=F32
    )
    modes = wide[:, :LANES] + wide[:, LANES:]
    modes = modes + jnp.dot(low_ref[...], high, preferred_element_type=F32)
    eighths = lax.broadcasted_iota(jnp.int32, (8, LANES), 0) * place_ref[0] % 8
    angle = eighths.astype(F32) * (2.0 * np.pi / 8)
    cosine = jnp.cos(angle)[None]
    sine = jnp.sin(angle)[None]
    turned = quarter_turn(modes).reshape(L // 8, 8, LANES)
    modes = modes.reshape(L // 8, 8, LANES) * cosine + turned * sine
    modes_ref[...] = modes.reshape(L, LANES)

    def step(i, carry):
        for u in range(8):
            j = i * 8 + u
            out_ref[pl.ds(j, 1), :] = modes_ref[pl.ds(order_ref[j], 1), :]
        return carry

    lax.fori_loop(0, L // 8, step, 0, unroll=4)


def project_kernel(
    order_ref, place_ref, rows_ref, sums_ref, beam_ref, keep_ref, send_ref, held, sems
):
    def fetch(k):
        return pltpu.make_async_copy(beam_ref.at[k], held.at[k], sems.at[k])

    for k in range(SLOTS):
        fetch(k).start()

    counts = jnp.broadcast_to(rows_ref[...], (8, OWNERS))
    before = lax.broadcasted_iota(jnp.int32, (OWNERS, OWNERS), 0)
    before = before < lax.broadcasted_iota(jnp.int32, (OWNERS, OWNERS), 1)
    starts = jnp.dot(
        counts.astype(F32).astype(BF16),
        before.astype(F32).astype(BF16),
        preferred_element_type=F32,
    )
    starts = starts.astype(jnp.int32)[:1]
    counts = counts[:1]

    total = sums_ref[pl.ds(0, SLOTS * INNER), :]
    for z in range(1, OUTER):
        total = total + sums_ref[pl.ds(z * SLOTS * INNER, SLOTS * INNER), :]
    low = low_lanes((8, LANES))
    with_re, with_im = [], []
    for j in range(INNER // 2):
        tile = total[8 * j : 8 * j + 8]
        rolled = pltpu.roll(tile, HALF, 1)
        re = jnp.where(low, tile, pltpu.roll(rolled, 4, 0))[:4]
        im = jnp.where(low, rolled, pltpu.roll(tile, 4, 0))[:4]
        with_re.append(jnp.concatenate([re, im], axis=0))
        with_im.append(jnp.concatenate([im, -re], axis=0))
    weights = jnp.concatenate(with_re + with_im, axis=1).astype(BF16)

    ells = lax.broadcasted_iota(jnp.int32, (1, L), 1)
    rows = [None] * 8
    for k in range(SLOTS):
        fetch(k).wait()
        plane = held[k].reshape(2 * held.shape[2], L)
        product = jnp.dot(weights, plane, preferred_element_type=F32)
        keep = ells >= order_ref[place_ref[0] * SLOTS + k]
        at = k // 2 * 4 + k % 2
        rows[at] = jnp.where(keep, product[k : k + 1], 0.0)
        rows[at + 2] = jnp.where(keep, product[4 + k : 5 + k], 0.0)
    alm = jnp.concatenate(rows, axis=0)
    alm = jnp.concatenate(list(split(alm)), axis=0)

    first = place_ref[1] == 0
    at = lax.broadcasted_iota(jnp.int32, (L, OWNERS), 0)
    for pair in range(ROWCAP // 2):
        picks = []
        for q in (2 * pair, 2 * pair + 1):
            wanted = jnp.where(counts > q, starts + q, -1)
            picks.append(jnp.where(at == wanted, 1.0, 0.0).astype(BF16))
        picked = jnp.dot(alm, jnp.concatenate(picks, axis=1), preferred_element_type=F32)
        picked = picked[:8] + picked[8:]
        for i in range(2):
            block = picked[:, i * OWNERS : (i + 1) * OWNERS]
            rows_at = pl.ds(2 * pair + i, 4, stride=ROWCAP)
            keep_ref[rows_at, :] = jnp.where(first, block[:4], block[4:])
            send_ref[rows_at, :] = jnp.where(first, block[4:], block[:4])


def call(kernel, out_shape, in_specs, scratch_shapes=()):
    return pl.pallas_call(
        kernel,
        out_shape=out_shape,
        in_specs=in_specs,
        out_specs=jax.tree.map(lambda _: VMEM, out_shape),
        scratch_shapes=scratch_shapes,
        compiler_params=pltpu.CompilerParams(vmem_limit_bytes=32 * 1024 * 1024),
    )


def body(vis, counts, m_order, beam, row_counts):
    outer = lax.axis_index("outer")
    inner = lax.axis_index("inner")
    core = lax.axis_index("bl")
    share = vis.shape[1]
    bases = vis.shape[2]
    high, low = transform_tables()

    packed = call(
        pack_kernel, jax.ShapeDtypeStruct((INNER, share, LANES), F32), [VMEM, VMEM]
    )(vis, counts.reshape(bases // LANES, LANES))
    gathered = lax.all_to_all(packed, "inner", 0, 0, tiled=True)

    modes = call(
        transform_kernel,
        jax.ShapeDtypeStruct((L, LANES), F32),
        [SMEM, SMEM, VMEM, VMEM, VMEM],
        [pltpu.VMEM((L, LANES), F32)],
    )(
        m_order,
        outer.astype(jnp.int32).reshape(1),
        gathered.reshape(SPAN, LANES),
        jnp.asarray(high),
        jnp.asarray(low),
    )
    sums = lax.all_to_all(
        modes.reshape(OWNERS, SLOTS, LANES), ("outer", "inner"), 0, 0, tiled=True
    )

    place = jnp.stack([outer * INNER + inner, core]).astype(jnp.int32)
    half = jax.ShapeDtypeStruct((4 * ROWCAP, OWNERS), F32)
    keep, send = call(
        project_kernel,
        (half, half),
        [SMEM, SMEM, VMEM, VMEM, ANY],
        [pltpu.VMEM(beam.shape, BF16), pltpu.SemaphoreType.DMA((SLOTS,))],
    )(
        m_order,
        place,
        row_counts.reshape(1, OWNERS),
        sums.reshape(OWNERS * SLOTS, LANES),
        beam,
    )
    picked = keep + lax.ppermute(send, "bl", [(0, 1), (1, 0)])
    received = lax.all_to_all(picked.T, ("outer", "inner"), 0, 0, tiled=True)
    return received.T.reshape(2, 2, ROWCAP, OWNERS).transpose(0, 3, 1, 2)


def solution(mesh):
    mesh = Mesh(mesh.devices.reshape(OUTER, INNER, 2), ("outer", "inner", "bl"))
    ma = ("outer", "inner")
    placed = (P(None, ma, "bl"), P("bl"), P(), P(ma, None, "bl", None), P())
    return jax.shard_map(
        body, mesh=mesh, in_specs=placed, out_specs=P(None, None, "bl", ma), check_vma=False
    )
```

time: 317 us -> 77.5 us (0.24)
  waiting for transfers between devices: 232 us -> 20.7 us
  matrix products: 24.2 us -> 0 us
  starting transfers between devices: 0.01 us -> 23.2 us
  blocking collectives: 33.3 us -> 16.3 us
  between operations: 14.3 us -> 0.05 us
  Pallas kernels: 0 us -> 6.44 us
  other arithmetic: 3.75 us -> 0.08 us
    unnamed x2 -> x0, waiting for transfers between devices: 232 us -> none
    dot_general x8 -> x0, matrix products: 24.2 us -> none  [the longest x1 3.67 us: sidereal(): jnp.dot(cosine, vis_re, precision=high)]
    all_to_all x0 -> x2, waiting for transfers between devices: none -> 19.9 us  [the longest x1 12.4 us: body(): lax.all_to_all(modes.reshape(OWNERS, SLOTS, LANES), ('outer', 'inner'), 0...]
    all_to_all x0 -> x2, starting transfers between devices: none -> 19.4 us  [the longest x1 11.9 us: body(): lax.all_to_all(modes.reshape(OWNERS, SLOTS, LANES), ('outer', 'inner'), 0...]
    psum x1 -> x0, blocking collectives: 10.5 us -> none  [body(): summed = lax.psum(partial_alm, 'bl')]
    unnamed x11 -> x16, local copies, waits for them, and re-layouts: 1.13 us -> 9.48 us
    all_to_all x1, blocking collectives: 22.8 us -> 16.3 us  [body(): received = lax.all_to_all(picked.T, ('outer', 'inner'), 0, 0, tiled=True)]
    pallas_call x0 -> x3, Pallas kernels: none -> 6.44 us  [the longest x1 3.08 us: body(): call(project_kernel, (half, half), [SMEM, SMEM, VMEM, VMEM, ANY], [pltpu....]
  transfers between devices with their start and end apart: 1 -> 3, of which waited for: 1 -> 3; matrix products, arithmetic and copies ran while one was open for 0% -> 0% of each run, Pallas kernels for 0% -> 0%
where the time goes in v1:
time: 77.5 us; the launch traced here: 77 us
  starting transfers between devices  23.2 us (30%)
  waiting for transfers between devices  20.7 us (27%)
  blocking collectives  16.3 us (21%)
  local copies, waits for them, and re-layouts  10.3 us (13%)
  Pallas kernels  6.44 us (8%)
    all_to_all x1, blocking collectives, body(): received = lax.all_to_all(picked.T, ('outer', 'inner'), 0, 0, tiled=True)  16.3 us
    all_to_all x1, waiting for transfers between devices, body(): lax.all_to_all(modes.reshape(OWNERS, SLOTS, LANES), ('outer', 'inner'), 0...  12.4 us
    all_to_all x1, starting transfers between devices, body(): lax.all_to_all(modes.reshape(OWNERS, SLOTS, LANES), ('outer', 'inner'), 0...  11.9 us
    unnamed x16, local copies, waits for them, and re-layouts  9.48 us
    all_to_all x1, starting transfers between devices, body(): gathered = lax.all_to_all(packed, 'inner', 0, 0, tiled=True)  7.58 us
    all_to_all x1, waiting for transfers between devices, body(): gathered = lax.all_to_all(packed, 'inner', 0, 0, tiled=True)  7.54 us
    ppermute x1, starting transfers between devices, body(): picked = keep + lax.ppermute(send, 'bl', [(0, 1), (1, 0)])  3.74 us
    pallas_call x1, Pallas kernels, body(): call(project_kernel, (half, half), [SMEM, SMEM, VMEM, VMEM, ANY], [pltpu....  3.08 us
  transfers between devices with their start and end apart: 3, of which 3 were waited for; matrix products, arithmetic and copies ran while one was open for 0% of the time, Pallas kernels for 0%

profile of v1, /device:TPU:1, one launch (start us, length us, event | category | flops | bytes accessed | tf_op | source)
XLA Modules:
  0.0 77.0 jit_solution(13272205516093870690)
XLA Ops:
  0.0 0.0 copy-start.3
  0.0 0.9 %copy-done.3 = f32[2,32,1024]{2,1,0:T(8,128)S(1)} copy-done((f32[2,32,1024]{2,1,0:T(8,128)S(1)}, f32[2,32,1024]{2,1,0:T(8,128)}, u32[]{:S(2)}) %copy-start.3) | copy-done | bytes 262168
  1.0 0.0 copy-start.6
  1.0 0.7 copy-done.6
  1.6 0.8 %shard_map.73 = f32[16,32,128]{2,1,0:T(8,128)} custom-call(f32[2,32,1024]{2,1,0:T(8,128)S(1)} %copy-done.3, s32[8,128]{1,0:T(8,128)S(1)} %bitcast.21), custom_call_target="tpu_custom_call" | custom-call | tf_op jit(solution)/shard_map/pallas_call | solution.py:170
  2.5 7.6 %all-to-all-start = ((f32[16,32,128]{2,1,0:T(8,128)}), f32[16,32,128]{2,1,0:T(8,128)S(1)}, u32[]{:S(2)}, u32[]{:S(2)}) async-start(f32[16,32,128]{2,1,0:T(8,128)} %shard_map.73), calls=%async_computation | async-start | bytes 524288 | tf_op jit(solution)/shard_map/all_to_all | solution.py:173
  10.1 7.5 %all-to-all-done = f32[16,32,128]{2,1,0:T(8,128)S(1)} async-done(((f32[16,32,128]{2,1,0:T(8,128)}), f32[16,32,128]{2,1,0:T(8,128)S(1)}, u32[]{:S(2)}, u32[]{:S(2)}) %all-to-all-start) | async-done | bytes 262176 | tf_op jit(solution)/shard_map/all_to_all | solution.py:173
  17.6 0.0 copy-start.1
  17.6 1.2 %copy-done.1 = bf16[512,1024]{1,0:T(8,128)(2,1)S(1)} copy-done((bf16[512,1024]{1,0:T(8,128)(2,1)S(1)}, bf16[512,1024]{1,0:T(8,128)(2,1)}, u32[]{:S(2)}) %copy-start.1) | copy-done | bytes 1048600
  18.8 1.2 %copy-done.2 = bf16[512,1024]{1,0:T(8,128)(2,1)S(1)} copy-done((bf16[512,1024]{1,0:T(8,128)(2,1)S(1)}, bf16[512,1024]{1,0:T(8,128)(2,1)}, u32[]{:S(2)}) %copy-start.2) | copy-done | bytes 1048600
  20.1 0.7 copy-done.4
  20.7 2.5 %shard_map.74 = f32[512,128]{1,0:T(8,128)} custom-call(s32[512]{0:T(512)S(1)} %copy-done.4, s32[1]{0:T(128)} %bitcast.3.place_ref, f32[512,128]{1,0:T(8,128)S(1)} %bitcast.20, bf16[512,1024]{1,0:T(8,128)(2,1)S(1)} %copy-done.2, bf16[512,1024]{1,0:T(8,128)(2,1)S(1)} %copy-done.1), custom_call_target="tpu_custom_call" | custom-call | tf_op jit(solution)/shard_map/pallas_call | solution.py:175
  23.3 11.9 %all-to-all-start.1 = ((f32[128,4,128]{2,1,0:T(4,128)}), f32[128,4,128]{2,1,0:T(4,128)S(1)}, u32[]{:S(2)}, u32[]{:S(2)}) async-start(f32[128,4,128]{2,1,0:T(4,128)} %bitcast.6), calls=%async_computation.1 | async-start | bytes 524288 | tf_op jit(solution)/shard_map/all_to_all | solution.py:187
  35.2 0.1 pad_add_fusion.place_ref
  35.2 12.4 %all-to-all-done.1 = f32[128,4,128]{2,1,0:T(4,128)S(1)} async-done(((f32[128,4,128]{2,1,0:T(4,128)}), f32[128,4,128]{2,1,0:T(4,128)S(1)}, u32[]{:S(2)}, u32[]{:S(2)}) %all-to-all-start.1) | async-done | bytes 262176 | tf_op jit(solution)/shard_map/all_to_all | solution.py:187
  47.6 3.4 %copy-done = bf16[4,2,1024,512]{3,2,1,0:T(8,128)(2,1)S(1)} copy-done((bf16[4,2,1024,512]{3,2,1,0:T(8,128)(2,1)S(1)}, bf16[4,2,1024,512]{3,2,1,0:T(8,128)(2,1)}, u32[]{:S(2)}) %copy-start) | copy-done | bytes 8388632
  51.0 0.7 copy-done.5
  51.7 0.7 copy-done.7
  52.3 3.1 %shard_map.75 = (f32[32,128]{1,0:T(8,128)S(1)}, f32[32,128]{1,0:T(8,128)S(1)}) custom-call(s32[512]{0:T(512)S(1)} %copy-done.5, s32[2]{0:T(128)S(1)} %pad_add_fusion.place_ref, s32[1,128]{1,0:T(1,128)S(1)} %bitcast.22, f32[512,128]{1,0:T(8,128)S(1)} %bitcast.19, bf16[4,2,1024,512]{3,2,1,0:T(8,128)(2,1)S(1)} %copy-done), custom_call_target="tpu_custom_call" | custom-call | tf_op jit(solution)/shard_map/pallas_call | solution.py:193
  55.4 3.7 %collective-permute-start = (f32[32,128]{1,0:T(8,128)S(1)}, f32[32,128]{1,0:T(8,128)S(1)}, u32[]{:S(2)}, u32[]{:S(2)}) collective-permute-start(f32[32,128]{1,0:T(8,128)S(1)} %get-tuple-element.8), channel_id=1, source_target_pairs={{0,1},{1,0},{2,3},{3,2},{4,5},{5,4},{6,7},{7,6},{8,9},{9,8},{10,11... | collective-permute-start | bytes 49160 | tf_op jit(solution)/shard_map/ppermute | solution.py:205
  59.1 0.8 %collective-permute-done = f32[32,128]{1,0:T(8,128)S(1)} collective-permute-done((f32[32,128]{1,0:T(8,128)S(1)}, f32[32,128]{1,0:T(8,128)S(1)}, u32[]{:S(2)}, u32[]{:S(2)}) %collective-permute-start) | collective-permute-done | bytes 16416 | tf_op jit(solution)/shard_map/ppermute | solution.py:205
  60.0 0.1 copy.10
  60.1 16.3 %all_to_all.22 = f32[128,1,32]{2,1,0:T(1,128)S(1)} all-to-all(f32[128,1,32]{2,1,0:T(1,128)S(1)} %copy.10), channel_id=1, replica_groups=mesh['outer'=8,'inner'=16,'bl'=2] {'outer','inner'}, dimensions={0} | all-to-all | bytes 32768 | tf_op jit(solution)/shard_map/all_to_all | solution.py:206
  76.3 0.7 copy.11
  (6 shorter events, 0.0 us)
Async XLA Ops:
  0.0 0.9 %copy-start.3 = (f32[2,32,1024]{2,1,0:T(8,128)S(1)}, f32[2,32,1024]{2,1,0:T(8,128)}, u32[]{:S(2)}) copy-start(f32[2,32,1024]{2,1,0:T(8,128)} %vis_ref.1) | copy-start | bytes 786436
  1.0 0.7 copy-start.6
  2.5 15.1 %all-to-all-start = ((f32[16,32,128]{2,1,0:T(8,128)}), f32[16,32,128]{2,1,0:T(8,128)S(1)}, u32[]{:S(2)}, u32[]{:S(2)}) async-start(f32[16,32,128]{2,1,0:T(8,128)} %shard_map.73), calls=%async_computation | async-start | bytes 524288 | tf_op jit(solution)/shard_map/all_to_all | solution.py:173
  17.6 1.2 %copy-start.1 = (bf16[512,1024]{1,0:T(8,128)(2,1)S(1)}, bf16[512,1024]{1,0:T(8,128)(2,1)}, u32[]{:S(2)}) copy-start(bf16[512,1024]{1,0:T(8,128)(2,1)} %constant.21.clone.low_ref) | copy-start | bytes 3145732
  18.8 1.2 %copy-start.2 = (bf16[512,1024]{1,0:T(8,128)(2,1)S(1)}, bf16[512,1024]{1,0:T(8,128)(2,1)}, u32[]{:S(2)}) copy-start(bf16[512,1024]{1,0:T(8,128)(2,1)} %constant.20.clone.high_ref) | copy-start | bytes 3145732
  20.1 0.7 copy-start.4
  23.3 24.3 %all-to-all-start.1 = ((f32[128,4,128]{2,1,0:T(4,128)}), f32[128,4,128]{2,1,0:T(4,128)S(1)}, u32[]{:S(2)}, u32[]{:S(2)}) async-start(f32[128,4,128]{2,1,0:T(4,128)} %bitcast.6), calls=%async_computation.1 | async-start | bytes 524288 | tf_op jit(solution)/shard_map/all_to_all | solution.py:187
  47.6 3.4 %copy-start = (bf16[4,2,1024,512]{3,2,1,0:T(8,128)(2,1)S(1)}, bf16[4,2,1024,512]{3,2,1,0:T(8,128)(2,1)}, u32[]{:S(2)}) copy-start(bf16[4,2,1024,512]{3,2,1,0:T(8,128)(2,1)} %beam_ref.1) | copy-start | bytes 25165828
  51.0 0.7 copy-start.5
  51.7 0.7 copy-start.7
  55.4 4.6 %collective-permute-start = (f32[32,128]{1,0:T(8,128)S(1)}, f32[32,128]{1,0:T(8,128)S(1)}, u32[]{:S(2)}, u32[]{:S(2)}) collective-permute-start(f32[32,128]{1,0:T(8,128)S(1)} %get-tuple-element.8), channel_id=1, source_target_pairs={{0,1},{1,0},{2,3},{3,2},{4,5},{5,4},{6,7},{7,6},{8,9},{9,8},{10,11... | collective-permute-start | bytes 49160 | tf_op jit(solution)/shard_map/ppermute | solution.py:205

commit v2 on v1

v2 whole, which is shorter than its diff:
```python
import numpy as np
import jax
import jax.numpy as jnp
from jax import lax
from jax.experimental import pallas as pl
from jax.experimental.pallas import tpu as pltpu
from jax.sharding import Mesh
from jax.sharding import PartitionSpec as P

L = 512
TIMES = 4096
OUTER = 8
INNER = 16
SPAN = TIMES // OUTER
OWNERS = OUTER * INNER
SLOTS = 4
ROWCAP = 8
LANES = 128
HALF = 64
PARTS = 4
HELD = 6

F32 = jnp.float32
BF16 = jnp.bfloat16
I32 = jnp.int32
VMEM = pl.BlockSpec(memory_space=pltpu.VMEM)
SMEM = pl.BlockSpec(memory_space=pltpu.SMEM)
HBM = pl.BlockSpec(memory_space=pltpu.HBM)


def transform_tables():
    turns = np.outer(np.arange(L), np.arange(SPAN)) % TIMES
    phase = 2.0 * np.pi / TIMES * turns
    table = np.concatenate([np.cos(phase), np.sin(phase)], axis=1) / np.sqrt(TIMES)
    table = table.astype(np.float32)
    high = table.astype(BF16)
    low = (table - high.astype(np.float32)).astype(BF16)
    return high, low


def low_lanes(shape):
    return lax.broadcasted_iota(I32, shape, 1) < HALF


def quarter_turn(pair):
    turned = pltpu.roll(pair, HALF, 1)
    return jnp.where(low_lanes(pair.shape), turned, -turned)


def split(array):
    high = array.astype(BF16)
    return high, (array - high.astype(F32)).astype(BF16)


def ones_where(condition):
    return jnp.where(condition, 1.0, 0.0).astype(BF16)


def pack_kernel(vis_ref, counts_ref, out_ref, vis, counts, packed, in_sems, out_sems, sem):
    blocks = vis.shape[0]
    weigh = pltpu.make_async_copy(counts_ref, counts, sem)
    weigh.start()

    def fetch(j):
        lanes = pl.ds(j * LANES, LANES)
        return pltpu.make_async_copy(vis_ref.at[:, :, lanes], vis.at[j], in_sems.at[j])

    def store(j):
        two = pl.ds(2 * j, 2)
        return pltpu.make_async_copy(packed.at[two], out_ref.at[two], out_sems.at[j])

    for j in range(blocks):
        fetch(j).start()
    weigh.wait()
    low = low_lanes(vis.shape[2:])
    for j in range(blocks):
        fetch(j).wait()
        scale = counts[j : j + 1, :].astype(F32) * (1.0 / 256.0)
        re = vis[j, 0] * scale
        im = vis[j, 1] * scale
        packed[2 * j] = jnp.where(low, re, pltpu.roll(im, HALF, 1))
        packed[2 * j + 1] = jnp.where(low, pltpu.roll(re, HALF, 1), im)
        store(j).start()
    for j in range(blocks):
        store(j).wait()


def tables_kernel(
    outer_ref, high_hbm, low_hbm, order_hbm, high_ref, low_ref, pick_ref, turn_ref, order, sems
):
    copies = [
        pltpu.make_async_copy(order_hbm, order.at[pl.ds(0, L // LANES)], sems.at[0]),
        pltpu.make_async_copy(high_hbm, high_ref, sems.at[1]),
        pltpu.make_async_copy(low_hbm, low_ref, sems.at[2]),
    ]
    for copy in copies:
        copy.start()
    eighths = lax.broadcasted_iota(I32, (8, LANES), 0) * outer_ref[0] % 8
    angle = eighths.astype(F32) * (2.0 * np.pi / 8)
    turn_ref[0] = jnp.cos(angle)
    turn_ref[1] = jnp.sin(angle)
    copies[0].wait()
    columns = order[...].T
    modes = lax.broadcasted_iota(I32, (LANES, L), 1)
    for i in range(L // LANES):
        pick_ref[i * LANES : (i + 1) * LANES, :] = ones_where(modes == columns[:, i : i + 1])
    copies[1].wait()
    copies[2].wait()


def transform_kernel(
    x_ref, high_ref, low_ref, pick_ref, turn_ref, out_ref, token_ref, slots_ref, sem
):
    x = x_ref[...]
    high, low = split(jnp.concatenate([x, quarter_turn(x)], axis=0))
    wide = jnp.dot(
        high_ref[...], jnp.concatenate([high, low], axis=1), preferred_element_type=F32
    )
    modes = wide[:, :LANES] + wide[:, LANES:]
    modes = modes + jnp.dot(low_ref[...], high, preferred_element_type=F32)
    turned = quarter_turn(modes).reshape(L // 8, 8, LANES)
    modes = modes.reshape(L // 8, 8, LANES) * turn_ref[0][None] + turned * turn_ref[1][None]
    parts = jnp.concatenate(split(modes.reshape(L, LANES)), axis=1)
    slots = jnp.dot(pick_ref[...], parts, preferred_element_type=F32)
    slots_ref[...] = slots[:, :LANES] + slots[:, LANES:]
    token_ref[...] = jnp.zeros_like(token_ref)
    store = pltpu.make_async_copy(slots_ref, out_ref, sem)
    store.start()
    store.wait()


def held_kernel(
    place_ref,
    token_ref,
    order_hbm,
    rows_hbm,
    beam_hbm,
    held_ref,
    wanted_ref,
    keep_ref,
    order,
    rows,
    sems,
):
    rows_copy = pltpu.make_async_copy(rows_hbm, rows, sems.at[0])
    order_copy = pltpu.make_async_copy(order_hbm, order, sems.at[1])
    held_copy = pltpu.make_async_copy(beam_hbm.at[pl.ds(0, HELD)], held_ref, sems.at[2])
    rows_copy.start()
    order_copy.start()
    held_copy.start()

    order_copy.wait()
    ells = lax.broadcasted_iota(I32, (1, L), 1)
    for k in range(SLOTS):
        keep = jnp.where(ells >= order[place_ref[0] * SLOTS + k], 1.0, 0.0)
        at = k // 2 * 4 + k % 2
        keep_ref[at : at + 1, :] = keep
        keep_ref[at + 2 : at + 3, :] = keep

    rows_copy.wait()
    before = lax.broadcasted_iota(I32, (OWNERS, OWNERS), 0)
    before = ones_where(before < lax.broadcasted_iota(I32, (OWNERS, OWNERS), 1))
    counts = jnp.broadcast_to(rows[...], (ROWCAP, OWNERS))
    starts = jnp.dot(counts.astype(F32).astype(BF16), before, preferred_element_type=F32)
    within = lax.broadcasted_iota(I32, (ROWCAP, OWNERS), 0)
    wanted_ref[...] = jnp.where(within < counts, starts.astype(I32) + within, -1)
    held_copy.wait()


def project_kernel(
    core_ref,
    sums_ref,
    held_ref,
    wanted_ref,
    keep_ref,
    beam_hbm,
    own_ref,
    other_ref,
    beam,
    pick,
    sems,
):
    def fetch(i):
        return pltpu.make_async_copy(beam_hbm.at[i], beam.at[i - HELD], sems.at[i - HELD])

    for i in range(HELD, SLOTS * PARTS):
        fetch(i).start()

    at = lax.broadcasted_iota(I32, (L, OWNERS), 0)
    for q in range(ROWCAP):
        wanted = wanted_ref[q : q + 1, :]
        pick[:, q * OWNERS : (q + 1) * OWNERS] = ones_where(at == wanted)

    total = sums_ref[pl.ds(0, SLOTS * INNER), :]
    for z in range(1, OUTER):
        total = total + sums_ref[pl.ds(z * SLOTS * INNER, SLOTS * INNER), :]
    low = low_lanes((8, LANES))
    with_re, with_im = [], []
    for j in range(INNER // 2):
        tile = total[8 * j : 8 * j + 8]
        rolled = pltpu.roll(tile, HALF, 1)
        re = jnp.where(low, tile, pltpu.roll(rolled, 4, 0))[:4]
        im = jnp.where(low, rolled, pltpu.roll(tile, 4, 0))[:4]
        with_re.append(jnp.concatenate([re, im], axis=0))
        with_im.append(jnp.concatenate([im, -re], axis=0))
    weights = jnp.concatenate(with_re + with_im, axis=1).astype(BF16)
    depth = weights.shape[1] // PARTS

    def product(i):
        if i < HELD:
            block = held_ref[i]
        else:
            fetch(i).wait()
            block = beam[i - HELD]
        part = i % PARTS * depth
        return jnp.dot(weights[:, part : part + depth], block, preferred_element_type=F32)

    alm = [None] * 8
    for k in range(SLOTS):
        both = sum(product(k * PARTS + part) for part in range(PARTS))
        at = k // 2 * 4 + k % 2
        alm[at] = both[k : k + 1]
        alm[at + 2] = both[4 + k : 5 + k]
    alm = jnp.where(keep_ref[...] > 0.0, jnp.concatenate(alm, axis=0), 0.0)
    alm = jnp.concatenate(split(alm), axis=0)

    wide = jnp.dot(alm, pick[...], preferred_element_type=F32)
    wide = wide[:8] + wide[8:]
    first = core_ref[0] == 0
    for q in range(ROWCAP):
        block = wide[:, q * OWNERS : (q + 1) * OWNERS]
        rows_at = pl.ds(q, 4, stride=ROWCAP)
        own_ref[rows_at, :] = jnp.where(first, block[:4], block[4:])
        other_ref[rows_at, :] = jnp.where(first, block[4:], block[:4])


def call(kernel, out_shape, in_specs, scratch_shapes=(), scoped=8):
    return pl.pallas_call(
        kernel,
        out_shape=out_shape,
        in_specs=in_specs,
        out_specs=jax.tree.map(lambda a: pl.BlockSpec(memory_space=a.memory_space), out_shape),
        scratch_shapes=scratch_shapes,
        compiler_params=pltpu.CompilerParams(vmem_limit_bytes=scoped * 1024 * 1024),
    )


def in_hbm(array):
    return pltpu.with_memory_space_constraint(array, pltpu.HBM)


def in_vmem(array):
    return pltpu.with_memory_space_constraint(array, pltpu.VMEM)


def body(vis, counts, m_order, beam, row_counts):
    outer = lax.axis_index("outer")
    inner = lax.axis_index("inner")
    core = lax.axis_index("bl")
    share = vis.shape[1]
    blocks = vis.shape[2] // LANES
    high, low = transform_tables()
    dma = pltpu.SemaphoreType.DMA

    packed = call(
        pack_kernel,
        pltpu.HBM((INNER, share, LANES), F32),
        [HBM, HBM],
        [
            pltpu.VMEM((blocks, 2, share, LANES), F32),
            pltpu.VMEM((blocks, LANES), I32),
            pltpu.VMEM((INNER, share, LANES), F32),
            dma((blocks,)),
            dma((blocks,)),
            dma(()),
        ],
    )(in_hbm(vis), in_hbm(counts.reshape(blocks, LANES)))
    gathered = lax.all_to_all(packed, "inner", 0, 0, tiled=True)

    tables = call(
        tables_kernel,
        (
            pltpu.VMEM(high.shape, BF16),
            pltpu.VMEM(low.shape, BF16),
            pltpu.VMEM((L, L), BF16),
            pltpu.VMEM((2, 8, LANES), F32),
        ),
        [SMEM, HBM, HBM, HBM],
        [pltpu.VMEM((8, LANES), I32), dma((3,))],
    )(
        outer.astype(I32).reshape(1),
        in_hbm(jnp.asarray(high)),
        in_hbm(jnp.asarray(low)),
        in_hbm(m_order.reshape(L // LANES, LANES)),
    )
    modes, token = call(
        transform_kernel,
        (pltpu.HBM((L, LANES), F32), pltpu.VMEM((8, LANES), F32)),
        [VMEM] * 5,
        [pltpu.VMEM((L, LANES), F32), dma(())],
    )(gathered.reshape(SPAN, LANES), *map(in_vmem, tables))
    sums = lax.all_to_all(
        modes.reshape(OWNERS, SLOTS, LANES), ("outer", "inner"), 0, 0, tiled=True
    )

    beam = in_hbm(beam.reshape(SLOTS * PARTS, -1, L))
    held = call(
        held_kernel,
        (
            pltpu.VMEM((HELD, *beam.shape[1:]), BF16),
            pltpu.VMEM((ROWCAP, OWNERS), I32),
            pltpu.VMEM((8, L), F32),
        ),
        [SMEM, VMEM, HBM, HBM, HBM],
        [pltpu.SMEM((L,), I32), pltpu.VMEM((1, OWNERS), I32), dma((3,))],
    )(
        (outer * INNER + inner).astype(I32).reshape(1),
        token,
        in_hbm(m_order),
        in_hbm(row_counts.reshape(1, OWNERS)),
        beam,
    )
    half = pltpu.VMEM((4 * ROWCAP, OWNERS), F32)
    streamed = SLOTS * PARTS - HELD
    own, other = call(
        project_kernel,
        (half, half),
        [SMEM] + [VMEM] * 4 + [HBM],
        [
            pltpu.VMEM((streamed, *beam.shape[1:]), BF16),
            pltpu.VMEM((L, ROWCAP * OWNERS), BF16),
            dma((streamed,)),
        ],
        scoped=24,
    )(
        core.astype(I32).reshape(1),
        sums.reshape(OWNERS * SLOTS, LANES),
        *map(in_vmem, held),
        beam,
    )
    picked = own + lax.ppermute(other, "bl", [(0, 1), (1, 0)])
    received = lax.all_to_all(picked.T, ("outer", "inner"), 0, 0, tiled=True)
    return received.T.reshape(2, 2, ROWCAP, OWNERS).transpose(0, 3, 1, 2)


def solution(mesh):
    mesh = Mesh(mesh.devices.reshape(OUTER, INNER, 2), ("outer", "inner", "bl"))
    ma = ("outer", "inner")
    placed = (P(None, ma, "bl"), P("bl"), P(), P(ma, None, "bl", None), P())
    return jax.shard_map(
        body, mesh=mesh, in_specs=placed, out_specs=P(None, None, "bl", ma), check_vma=False
    )
```

time: 77.5 us -> 69.1 us (0.89)
  local copies, waits for them, and re-layouts: 10.3 us -> 0.78 us
  Pallas kernels: 6.44 us -> 11.1 us
  waiting for transfers between devices: 20.7 us -> 17.3 us
    unnamed x16 -> x0, local copies, waits for them, and re-layouts: 9.48 us -> none
    pallas_call x3 -> x5, Pallas kernels: 6.44 us -> 11.1 us  [the longest x1 3.43 us: body(): call(project_kernel, (half, half), [SMEM] + [VMEM] * 4 + [HBM], [pltpu.VM...]
    all_to_all x1, waiting for transfers between devices: 12.4 us -> 10.5 us  [body(): lax.all_to_all(modes.reshape(OWNERS, SLOTS, LANES), ('outer', 'inner'), 0...]
    all_to_all x1, waiting for transfers between devices: 7.54 us -> 5.94 us  [body(): gathered = lax.all_to_all(packed, 'inner', 0, 0, tiled=True)]
  transfers between devices with their start and end apart: 3 -> 3, of which waited for: 3 -> 3; matrix products, arithmetic and copies ran while one was open for 0% -> 0% of each run, Pallas kernels for 0% -> 5%
where the time goes in v2:
time: 69.1 us; the launch traced here: 68.7 us
  starting transfers between devices  23.2 us (34%)
  waiting for transfers between devices  17.3 us (25%)
  blocking collectives  16.3 us (24%)
  Pallas kernels  11.1 us (16%)
  local copies, waits for them, and re-layouts  0.78 us (1%)
    all_to_all x1, blocking collectives, body(): received = lax.all_to_all(picked.T, ('outer', 'inner'), 0, 0, tiled=True)  16.3 us
    all_to_all x1, starting transfers between devices, body(): lax.all_to_all(modes.reshape(OWNERS, SLOTS, LANES), ('outer', 'inner'), 0...  11.9 us
    all_to_all x1, waiting for transfers between devices, body(): lax.all_to_all(modes.reshape(OWNERS, SLOTS, LANES), ('outer', 'inner'), 0...  10.5 us
    all_to_all x1, starting transfers between devices, body(): gathered = lax.all_to_all(packed, 'inner', 0, 0, tiled=True)  7.6 us
    all_to_all x1, waiting for transfers between devices, body(): gathered = lax.all_to_all(packed, 'inner', 0, 0, tiled=True)  5.94 us
    ppermute x1, starting transfers between devices, body(): picked = own + lax.ppermute(other, 'bl', [(0, 1), (1, 0)])  3.74 us
    pallas_call x1, Pallas kernels, body(): call(project_kernel, (half, half), [SMEM] + [VMEM] * 4 + [HBM], [pltpu.VM...  3.43 us
    pallas_call x1, Pallas kernels, body(): call(pack_kernel, pltpu.HBM((INNER, share, LANES), F32), [HBM, HBM], [plt...  2.2 us
  transfers between devices with their start and end apart: 3, of which 3 were waited for; matrix products, arithmetic and copies ran while one was open for 0% of the time, Pallas kernels for 5%

profile of v2, /device:TPU:1, one launch (start us, length us, event | category | flops | bytes accessed | tf_op | source)
XLA Modules:
  0.0 68.7 jit_solution(9991724639555109694)
XLA Ops:
  0.0 2.2 %shard_map.73 = f32[16,32,128]{2,1,0:T(8,128)} custom-call(f32[2,32,1024]{2,1,0:T(8,128)} %vis_ref.1, s32[8,128]{1,0:T(8,128)} %bitcast.27), custom_call_target="tpu_custom_call" | custom-call | tf_op jit(solution)/shard_map/pallas_call | solution.py:265
  2.2 7.6 %all-to-all-start = ((f32[16,32,128]{2,1,0:T(8,128)}), f32[16,32,128]{2,1,0:T(8,128)S(1)}, u32[]{:S(2)}, u32[]{:S(2)}) async-start(f32[16,32,128]{2,1,0:T(8,128)} %shard_map.73), calls=%async_computation | async-start | bytes 524288 | tf_op jit(solution)/shard_map/all_to_all | solution.py:278
  9.8 1.6 %shard_map.74 = (bf16[512,1024]{1,0:T(8,128)(2,1)S(1)}, bf16[512,1024]{1,0:T(8,128)(2,1)S(1)}, bf16[512,512]{1,0:T(8,128)(2,1)S(1)}, f32[2,8,128]{2,1,0:T(8,128)S(1)}) custom-call(s32[1]{0:T(128)} %bitcast.3.outer_ref, bf16[512,1024]{1,0:T(8,128)(2,1)} %constant.20.clone.high_hbm, bf16[512,1024]{1,0:T(8,128)(2,1)} %constant.21.clone.low_hbm, s32[4,128]{1,0:T(4,128)} %bitcast.26), custom_call_target="tpu_custom_call" | custom-call | tf_op jit(solution)/shard_map/pallas_call | solution.py:280
  11.4 5.9 %all-to-all-done = f32[16,32,128]{2,1,0:T(8,128)S(1)} async-done(((f32[16,32,128]{2,1,0:T(8,128)}), f32[16,32,128]{2,1,0:T(8,128)S(1)}, u32[]{:S(2)}, u32[]{:S(2)}) %all-to-all-start) | async-done | bytes 262176 | tf_op jit(solution)/shard_map/all_to_all | solution.py:278
  17.4 2.0 %shard_map.75 = (f32[512,128]{1,0:T(8,128)}, f32[8,128]{1,0:T(8,128)S(1)}) custom-call(f32[512,128]{1,0:T(8,128)S(1)} %bitcast.22, bf16[512,1024]{1,0:T(8,128)(2,1)S(1)} %get-tuple-element.16.high_ref, bf16[512,1024]{1,0:T(8,128)(2,1)S(1)} %get-tuple-element.17.low_ref, bf16[512,512]{1,0:T(8,128)(2,1)S(1)} %get-tuple-element.18.pick_ref, ...), custom_call_target="tpu_custom_call" | custom-call | tf_op jit(solution)/shard_map/pallas_call | solution.py:296
  19.3 11.9 %all-to-all-start.1 = ((f32[128,4,128]{2,1,0:T(4,128)}), f32[128,4,128]{2,1,0:T(4,128)S(1)}, u32[]{:S(2)}, u32[]{:S(2)}) async-start(f32[128,4,128]{2,1,0:T(4,128)} %bitcast.25), calls=%async_computation.1 | async-start | bytes 524288 | tf_op jit(solution)/shard_map/all_to_all | solution.py:302
  31.2 1.9 %shard_map.76 = (bf16[6,512,512]{2,1,0:T(8,128)(2,1)S(1)}, s32[8,128]{1,0:T(8,128)S(1)}, f32[8,512]{1,0:T(8,128)S(1)}) custom-call(s32[1]{0:T(128)} %bitcast.7.place_ref, f32[8,128]{1,0:T(8,128)S(1)} %get-tuple-element.21.token_ref, s32[512]{0:T(512)} %order_hbm.1, s32[1,128]{1,0:T(1,128)} %bitcast.28, bf16[16,512,512]{2,1,0:T(8,128)(2,1)} %bitcast.23), custom_call_target="tpu_custom_call" | custom-call | tf_op jit(solution)/shard_map/pallas_call | solution.py:307
  33.2 10.5 %all-to-all-done.1 = f32[128,4,128]{2,1,0:T(4,128)S(1)} async-done(((f32[128,4,128]{2,1,0:T(4,128)}), f32[128,4,128]{2,1,0:T(4,128)S(1)}, u32[]{:S(2)}, u32[]{:S(2)}) %all-to-all-start.1) | async-done | bytes 262176 | tf_op jit(solution)/shard_map/all_to_all | solution.py:302
  43.7 3.4 %shard_map.77 = (f32[32,128]{1,0:T(8,128)S(1)}, f32[32,128]{1,0:T(8,128)S(1)}) custom-call(s32[1]{0:T(128)} %bitcast.core_ref, f32[512,128]{1,0:T(8,128)S(1)} %bitcast.21, bf16[6,512,512]{2,1,0:T(8,128)(2,1)S(1)} %get-tuple-element.22.held_ref, s32[8,128]{1,0:T(8,128)S(1)} %get-tuple-element.23.wanted_ref, f32[8,512]{1,0:T(8,128)S(1)} %get-tuple-element.24.keep_ref, ...), custom_call_target="tpu_custom_call" | custom-call | tf_op jit(solution)/shard_map/pallas_call | solution.py:325
  47.1 3.7 %collective-permute-start = (f32[32,128]{1,0:T(8,128)S(1)}, f32[32,128]{1,0:T(8,128)S(1)}, u32[]{:S(2)}, u32[]{:S(2)}) collective-permute-start(f32[32,128]{1,0:T(8,128)S(1)} %get-tuple-element.26), channel_id=1, source_target_pairs={{0,1},{1,0},{2,3},{3,2},{4,5},{5,4},{6,7},{7,6},{8,9},{9,8},{10,11... | collective-permute-start | bytes 49160 | tf_op jit(solution)/shard_map/ppermute | solution.py:341
  50.8 0.8 %collective-permute-done = f32[32,128]{1,0:T(8,128)S(1)} collective-permute-done((f32[32,128]{1,0:T(8,128)S(1)}, f32[32,128]{1,0:T(8,128)S(1)}, u32[]{:S(2)}, u32[]{:S(2)}) %collective-permute-start) | collective-permute-done | bytes 16416 | tf_op jit(solution)/shard_map/ppermute | solution.py:341
  51.7 0.1 copy.10
  51.8 16.3 %all_to_all.22 = f32[128,1,32]{2,1,0:T(1,128)S(1)} all-to-all(f32[128,1,32]{2,1,0:T(1,128)S(1)} %copy.10), channel_id=1, replica_groups=mesh['outer'=8,'inner'=16,'bl'=2] {'outer','inner'}, dimensions={0} | all-to-all | bytes 32768 | tf_op jit(solution)/shard_map/all_to_all | solution.py:342
  68.1 0.7 copy.11
  (1 shorter events, 0.0 us)
Async XLA Ops:
  2.2 15.1 %all-to-all-start = ((f32[16,32,128]{2,1,0:T(8,128)}), f32[16,32,128]{2,1,0:T(8,128)S(1)}, u32[]{:S(2)}, u32[]{:S(2)}) async-start(f32[16,32,128]{2,1,0:T(8,128)} %shard_map.73), calls=%async_computation | async-start | bytes 524288 | tf_op jit(solution)/shard_map/all_to_all | solution.py:278
  19.3 24.3 %all-to-all-start.1 = ((f32[128,4,128]{2,1,0:T(4,128)}), f32[128,4,128]{2,1,0:T(4,128)S(1)}, u32[]{:S(2)}, u32[]{:S(2)}) async-start(f32[128,4,128]{2,1,0:T(4,128)} %bitcast.25), calls=%async_computation.1 | async-start | bytes 524288 | tf_op jit(solution)/shard_map/all_to_all | solution.py:302
  47.1 4.6 %collective-permute-start = (f32[32,128]{1,0:T(8,128)S(1)}, f32[32,128]{1,0:T(8,128)S(1)}, u32[]{:S(2)}, u32[]{:S(2)}) collective-permute-start(f32[32,128]{1,0:T(8,128)S(1)} %get-tuple-element.26), channel_id=1, source_target_pairs={{0,1},{1,0},{2,3},{3,2},{4,5},{5,4},{6,7},{7,6},{8,9},{9,8},{10,11... | collective-permute-start | bytes 49160 | tf_op jit(solution)/shard_map/ppermute | solution.py:341

commit v3 on v2

--- a/solution.py
+++ b/solution.py
@@ -4,7 +4,6 @@
 from jax import lax
 from jax.experimental import pallas as pl
 from jax.experimental.pallas import tpu as pltpu
-from jax.sharding import Mesh
 from jax.sharding import PartitionSpec as P
 
 L = 512
@@ -19,6 +18,10 @@
 HALF = 64
 PARTS = 4
 HELD = 6
+FIRST_INNER = 10
+FIRST_OUTER = 5
+FIRST = FIRST_OUTER * INNER + FIRST_INNER
+FIRST_LAST = FIRST
 
 F32 = jnp.float32
 BF16 = jnp.bfloat16
@@ -29,7 +32,8 @@
 
 
 def transform_tables():
-    turns = np.outer(np.arange(L), np.arange(SPAN)) % TIMES
+    times = np.arange(SPAN).reshape(INNER, -1)[np.arange(INNER) ^ FIRST_INNER]
+    turns = np.outer(np.arange(L), times) % TIMES
     phase = 2.0 * np.pi / TIMES * turns
     table = np.concatenate([np.cos(phase), np.sin(phase)], axis=1) / np.sqrt(TIMES)
     table = table.astype(np.float32)
@@ -50,6 +54,16 @@
 def split(array):
     high = array.astype(BF16)
     return high, (array - high.astype(F32)).astype(BF16)
+
+
+def lane_xor(array, mask):
+    lane = lax.broadcasted_iota(I32, array.shape, 1)
+    for bit in range(7):
+        step = 1 << bit
+        if mask & step:
+            up = pltpu.roll(array, LANES - step, 1)
+            array = jnp.where(lane & step == 0, up, pltpu.roll(array, step, 1))
+    return array
 
 
 def ones_where(condition):
@@ -100,10 +114,13 @@
     turn_ref[0] = jnp.cos(angle)
     turn_ref[1] = jnp.sin(angle)
     copies[0].wait()
-    columns = order[...].T
+    columns = lane_xor(order[...], SLOTS * FIRST % LANES).T
     modes = lax.broadcasted_iota(I32, (LANES, L), 1)
     for i in range(L // LANES):
-        pick_ref[i * LANES : (i + 1) * LANES, :] = ones_where(modes == columns[:, i : i + 1])
+        block = i ^ SLOTS * FIRST // LANES
+        pick_ref[i * LANES : (i + 1) * LANES, :] = ones_where(
+            modes == columns[:, block : block + 1]
+        )
     copies[1].wait()
     copies[2].wait()
 
@@ -158,10 +175,12 @@
         keep_ref[at + 2 : at + 3, :] = keep
 
     rows_copy.wait()
-    before = lax.broadcasted_iota(I32, (OWNERS, OWNERS), 0)
-    before = ones_where(before < lax.broadcasted_iota(I32, (OWNERS, OWNERS), 1))
-    counts = jnp.broadcast_to(rows[...], (ROWCAP, OWNERS))
-    starts = jnp.dot(counts.astype(F32).astype(BF16), before, preferred_element_type=F32)
+    counts = jnp.broadcast_to(rows[...], (ROWCAP, OWNERS)).astype(F32).astype(BF16)
+    other = lax.broadcasted_iota(I32, (OWNERS, OWNERS), 0)
+    owner = lax.broadcasted_iota(I32, (OWNERS, OWNERS), 1) ^ FIRST_LAST
+    starts = jnp.dot(counts, ones_where(other < owner), preferred_element_type=F32)
+    counts = jnp.dot(counts, ones_where(other == owner), preferred_element_type=F32)
+    counts = counts.astype(I32)
     within = lax.broadcasted_iota(I32, (ROWCAP, OWNERS), 0)
     wanted_ref[...] = jnp.where(within < counts, starts.astype(I32) + within, -1)
     held_copy.wait()
@@ -234,12 +253,25 @@
         other_ref[rows_at, :] = jnp.where(first, block[4:], block[:4])
 
 
+def finish_kernel(parts_ref, out_ref):
+    out_ref[...] = lane_xor(parts_ref[...].T, FIRST_LAST)
+
+
+def exchange(array, first, size):
+    groups = [
+        [base + (rank ^ first) for rank in range(size)] for base in range(0, OWNERS, size)
+    ]
+    return lax.all_to_all(array, "ma", 0, 0, axis_index_groups=groups, tiled=True)
+
+
 def call(kernel, out_shape, in_specs, scratch_shapes=(), scoped=8):
     return pl.pallas_call(
         kernel,
         out_shape=out_shape,
         in_specs=in_specs,
-        out_specs=jax.tree.map(lambda a: pl.BlockSpec(memory_space=a.memory_space), out_shape),
+        out_specs=jax.tree.map(
+            lambda a: pl.BlockSpec(memory_space=getattr(a, "memory_space", pltpu.VMEM)), out_shape
+        ),
         scratch_shapes=scratch_shapes,
         compiler_params=pltpu.CompilerParams(vmem_limit_bytes=scoped * 1024 * 1024),
     )
@@ -254,8 +286,7 @@
 
 
 def body(vis, counts, m_order, beam, row_counts):
-    outer = lax.axis_index("outer")
-    inner = lax.axis_index("inner")
+    place = lax.axis_index("ma")
     core = lax.axis_index("bl")
     share = vis.shape[1]
     blocks = vis.shape[2] // LANES
@@ -275,7 +306,7 @@
             dma(()),
         ],
     )(in_hbm(vis), in_hbm(counts.reshape(blocks, LANES)))
-    gathered = lax.all_to_all(packed, "inner", 0, 0, tiled=True)
+    gathered = exchange(packed, FIRST_INNER, INNER)
 
     tables = call(
         tables_kernel,
@@ -288,7 +319,7 @@
         [SMEM, HBM, HBM, HBM],
         [pltpu.VMEM((8, LANES), I32), dma((3,))],
     )(
-        outer.astype(I32).reshape(1),
+        (place // INNER).astype(I32).reshape(1),
         in_hbm(jnp.asarray(high)),
         in_hbm(jnp.asarray(low)),
         in_hbm(m_order.reshape(L // LANES, LANES)),
@@ -299,9 +330,7 @@
         [VMEM] * 5,
         [pltpu.VMEM((L, LANES), F32), dma(())],
     )(gathered.reshape(SPAN, LANES), *map(in_vmem, tables))
-    sums = lax.all_to_all(
-        modes.reshape(OWNERS, SLOTS, LANES), ("outer", "inner"), 0, 0, tiled=True
-    )
+    sums = exchange(modes.reshape(OWNERS, SLOTS, LANES), FIRST, OWNERS)
 
     beam = in_hbm(beam.reshape(SLOTS * PARTS, -1, L))
     held = call(
@@ -314,7 +343,7 @@
         [SMEM, VMEM, HBM, HBM, HBM],
         [pltpu.SMEM((L,), I32), pltpu.VMEM((1, OWNERS), I32), dma((3,))],
     )(
-        (outer * INNER + inner).astype(I32).reshape(1),
+        place.astype(I32).reshape(1),
         token,
         in_hbm(m_order),
         in_hbm(row_counts.reshape(1, OWNERS)),
@@ -339,14 +368,13 @@
         beam,
     )
     picked = own + lax.ppermute(other, "bl", [(0, 1), (1, 0)])
-    received = lax.all_to_all(picked.T, ("outer", "inner"), 0, 0, tiled=True)
-    return received.T.reshape(2, 2, ROWCAP, OWNERS).transpose(0, 3, 1, 2)
+    received = exchange(picked.T, FIRST_LAST, OWNERS)
+    out = call(finish_kernel, jax.ShapeDtypeStruct((4 * ROWCAP, OWNERS), F32), [VMEM])(received)
+    return out.reshape(2, 2, ROWCAP, OWNERS).transpose(0, 3, 1, 2)
 
 
 def solution(mesh):
-    mesh = Mesh(mesh.devices.reshape(OUTER, INNER, 2), ("outer", "inner", "bl"))
-    ma = ("outer", "inner")
-    placed = (P(None, ma, "bl"), P("bl"), P(), P(ma, None, "bl", None), P())
+    placed = (P(None, "ma", "bl"), P("bl"), P(), P("ma", None, "bl", None), P())
     return jax.shard_map(
-        body, mesh=mesh, in_specs=placed, out_specs=P(None, None, "bl", ma), check_vma=False
-    )
+        body, mesh=mesh, in_specs=placed, out_specs=P(None, None, "bl", "ma"), check_vma=False
+    )

time: 69.1 us -> 63.4 us (0.918)
  waiting for transfers between devices: 17.3 us -> 7.01 us
  starting transfers between devices: 23.2 us -> 27.6 us
  Pallas kernels: 11.1 us -> 12.1 us
    all_to_all x2, waiting for transfers between devices: 16.4 us -> 6.17 us  [exchange(): lax.all_to_all(array, 'ma', 0, 0, axis_index_groups=groups, tiled=True)]
    all_to_all x2, starting transfers between devices: 19.5 us -> 25.3 us  [exchange(): lax.all_to_all(array, 'ma', 0, 0, axis_index_groups=groups, tiled=True)]
    ppermute x1, starting transfers between devices: 3.74 us -> 2.29 us  [body(): picked = own + lax.ppermute(other, 'bl', [(0, 1), (1, 0)])]
    pallas_call x0 -> x1, Pallas kernels: none -> 0.96 us  [body(): call(finish_kernel, jax.ShapeDtypeStruct((4 * ROWCAP, OWNERS), F32), [VMEM])]
  transfers between devices with their start and end apart: 3 -> 3, of which waited for: 3 -> 3; matrix products, arithmetic and copies ran while one was open for 0% -> 0% of each run, Pallas kernels for 5% -> 6%
where the time goes in v3:
time: 63.4 us; the launch traced here: 63 us
  starting transfers between devices  27.6 us (44%)
  blocking collectives  16.1 us (25%)
  Pallas kernels  12.1 us (19%)
  waiting for transfers between devices  7.01 us (11%)
    all_to_all x2, starting transfers between devices, exchange(): lax.all_to_all(array, 'ma', 0, 0, axis_index_groups=groups, tiled=True)  25.3 us
    all_to_all x1, blocking collectives, exchange(): lax.all_to_all(array, 'ma', 0, 0, axis_index_groups=groups, tiled=True)  16.1 us
    all_to_all x2, waiting for transfers between devices, exchange(): lax.all_to_all(array, 'ma', 0, 0, axis_index_groups=groups, tiled=True)  6.17 us
    pallas_call x1, Pallas kernels, body(): call(project_kernel, (half, half), [SMEM] + [VMEM] * 4 + [HBM], [pltpu.VM...  3.43 us
    ppermute x1, starting transfers between devices, body(): picked = own + lax.ppermute(other, 'bl', [(0, 1), (1, 0)])  2.29 us
    pallas_call x1, Pallas kernels, body(): call(pack_kernel, pltpu.HBM((INNER, share, LANES), F32), [HBM, HBM], [plt...  2.2 us
    pallas_call x1, Pallas kernels, body(): call(transform_kernel, (pltpu.HBM((L, LANES), F32), pltpu.VMEM((8, LANES)...  1.96 us
    pallas_call x1, Pallas kernels, body(): call(held_kernel, (pltpu.VMEM((HELD, *beam.shape[1:]), BF16), pltpu.VMEM(...  1.94 us
  transfers between devices with their start and end apart: 3, of which 3 were waited for; matrix products, arithmetic and copies ran while one was open for 0% of the time, Pallas kernels for 6%

profile of v3, /device:TPU:1, one launch (start us, length us, event | category | flops | bytes accessed | tf_op | source)
XLA Modules:
  0.0 63.0 jit_solution(7361707831768969967)
XLA Ops:
  0.0 2.2 %shard_map.73 = f32[16,32,128]{2,1,0:T(8,128)} custom-call(f32[2,32,1024]{2,1,0:T(8,128)} %vis_ref.1, s32[8,128]{1,0:T(8,128)} %bitcast.25), custom_call_target="tpu_custom_call" | custom-call | tf_op jit(solution)/shard_map/pallas_call | solution.py:296
  2.2 9.6 %all-to-all-start = ((f32[16,32,128]{2,1,0:T(8,128)}), f32[16,32,128]{2,1,0:T(8,128)S(1)}, u32[]{:S(2)}, u32[]{:S(2)}) async-start(f32[16,32,128]{2,1,0:T(8,128)} %shard_map.73), calls=%async_computation | async-start | bytes 524288 | tf_op jit(solution)/shard_map/all_to_all | solution.py:264
  11.8 1.6 %shard_map.74 = (bf16[512,1024]{1,0:T(8,128)(2,1)S(1)}, bf16[512,1024]{1,0:T(8,128)(2,1)S(1)}, bf16[512,512]{1,0:T(8,128)(2,1)S(1)}, f32[2,8,128]{2,1,0:T(8,128)S(1)}) custom-call(s32[1]{0:T(128)} %bitcast.3.outer_ref, bf16[512,1024]{1,0:T(8,128)(2,1)} %constant.28.clone.high_hbm, bf16[512,1024]{1,0:T(8,128)(2,1)} %constant.29.clone.low_hbm, s32[4,128]{1,0:T(4,128)} %bitcast.24), custom_call_target="tpu_custom_call" | custom-call | tf_op jit(solution)/shard_map/pallas_call | solution.py:311
  13.4 2.6 %all-to-all-done = f32[16,32,128]{2,1,0:T(8,128)S(1)} async-done(((f32[16,32,128]{2,1,0:T(8,128)}), f32[16,32,128]{2,1,0:T(8,128)S(1)}, u32[]{:S(2)}, u32[]{:S(2)}) %all-to-all-start) | async-done | bytes 262176 | tf_op jit(solution)/shard_map/all_to_all | solution.py:264
  16.0 2.0 %shard_map.75 = (f32[512,128]{1,0:T(8,128)}, f32[8,128]{1,0:T(8,128)S(1)}) custom-call(f32[512,128]{1,0:T(8,128)S(1)} %bitcast.19, bf16[512,1024]{1,0:T(8,128)(2,1)S(1)} %get-tuple-element.16.high_ref, bf16[512,1024]{1,0:T(8,128)(2,1)S(1)} %get-tuple-element.17.low_ref, bf16[512,512]{1,0:T(8,128)(2,1)S(1)} %get-tuple-element.18.pick_ref, ...), custom_call_target="tpu_custom_call" | custom-call | tf_op jit(solution)/shard_map/pallas_call | solution.py:327
  18.0 15.7 %all-to-all-start.1 = ((f32[128,4,128]{2,1,0:T(4,128)}), f32[128,4,128]{2,1,0:T(4,128)S(1)}, u32[]{:S(2)}, u32[]{:S(2)}) async-start(f32[128,4,128]{2,1,0:T(4,128)} %bitcast.23), calls=%async_computation.1 | async-start | bytes 524288 | tf_op jit(solution)/shard_map/all_to_all | solution.py:264
  33.7 1.9 %shard_map.76 = (bf16[6,512,512]{2,1,0:T(8,128)(2,1)S(1)}, s32[8,128]{1,0:T(8,128)S(1)}, f32[8,512]{1,0:T(8,128)S(1)}) custom-call(s32[1]{0:T(128)} %bitcast.7.place_ref, f32[8,128]{1,0:T(8,128)S(1)} %get-tuple-element.21.token_ref, s32[512]{0:T(512)} %order_hbm.1, s32[1,128]{1,0:T(1,128)} %bitcast.26, bf16[16,512,512]{2,1,0:T(8,128)(2,1)} %bitcast.21), custom_call_target="tpu_custom_call" | custom-call | tf_op jit(solution)/shard_map/pallas_call | solution.py:336
  35.6 3.6 %all-to-all-done.1 = f32[128,4,128]{2,1,0:T(4,128)S(1)} async-done(((f32[128,4,128]{2,1,0:T(4,128)}), f32[128,4,128]{2,1,0:T(4,128)S(1)}, u32[]{:S(2)}, u32[]{:S(2)}) %all-to-all-start.1) | async-done | bytes 262176 | tf_op jit(solution)/shard_map/all_to_all | solution.py:264
  39.2 3.4 %shard_map.77 = (f32[32,128]{1,0:T(8,128)S(1)}, f32[32,128]{1,0:T(8,128)S(1)}) custom-call(s32[1]{0:T(128)} %bitcast.core_ref, f32[512,128]{1,0:T(8,128)S(1)} %bitcast.18, bf16[6,512,512]{2,1,0:T(8,128)(2,1)S(1)} %get-tuple-element.22.held_ref, s32[8,128]{1,0:T(8,128)S(1)} %get-tuple-element.23.wanted_ref, f32[8,512]{1,0:T(8,128)S(1)} %get-tuple-element.24.keep_ref, ...), custom_call_target="tpu_custom_call" | custom-call | tf_op jit(solution)/shard_map/pallas_call | solution.py:354
  42.6 2.3 %collective-permute-start = (f32[32,128]{1,0:T(8,128)S(1)}, f32[32,128]{1,0:T(8,128)S(1)}, u32[]{:S(2)}, u32[]{:S(2)}) collective-permute-start(f32[32,128]{1,0:T(8,128)S(1)} %get-tuple-element.26), channel_id=1, source_target_pairs={{0,1},{1,0},{2,3},{3,2},{4,5},{5,4},{6,7},{7,6},{8,9},{9,8},{10,11... | collective-permute-start | bytes 49160 | tf_op jit(solution)/shard_map/ppermute | solution.py:370
  44.9 0.8 %collective-permute-done = f32[32,128]{1,0:T(8,128)S(1)} collective-permute-done((f32[32,128]{1,0:T(8,128)S(1)}, f32[32,128]{1,0:T(8,128)S(1)}, u32[]{:S(2)}, u32[]{:S(2)}) %collective-permute-start) | collective-permute-done | bytes 16416 | tf_op jit(solution)/shard_map/ppermute | solution.py:370
  45.8 0.1 copy.10
  45.9 16.1 %all_to_all.21 = f32[128,1,32]{2,1,0:T(1,128)S(1)} all-to-all(f32[128,1,32]{2,1,0:T(1,128)S(1)} %copy.10), channel_id=1, replica_groups={{180,182,176,178,188,190,184,186,164,166,160,162,172,174,168,170,148,15..., dimensions={0} | all-to-all | bytes 32768 | tf_op jit(solution)/shard_map/all_to_all | solution.py:264
  62.0 1.0 %shard_map.78 = f32[32,128]{1,0:T(8,128)} custom-call(f32[128,32]{1,0:T(8,128)S(1)} %bitcast.20), custom_call_target="tpu_custom_call" | custom-call | tf_op jit(solution)/shard_map/pallas_call | solution.py:372
  (1 shorter events, 0.0 us)
Async XLA Ops:
  2.2 13.8 %all-to-all-start = ((f32[16,32,128]{2,1,0:T(8,128)}), f32[16,32,128]{2,1,0:T(8,128)S(1)}, u32[]{:S(2)}, u32[]{:S(2)}) async-start(f32[16,32,128]{2,1,0:T(8,128)} %shard_map.73), calls=%async_computation | async-start | bytes 524288 | tf_op jit(solution)/shard_map/all_to_all | solution.py:264
  18.0 21.2 %all-to-all-start.1 = ((f32[128,4,128]{2,1,0:T(4,128)}), f32[128,4,128]{2,1,0:T(4,128)S(1)}, u32[]{:S(2)}, u32[]{:S(2)}) async-start(f32[128,4,128]{2,1,0:T(4,128)} %bitcast.23), calls=%async_computation.1 | async-start | bytes 524288 | tf_op jit(solution)/shard_map/all_to_all | solution.py:264
  42.6 3.1 %collective-permute-start = (f32[32,128]{1,0:T(8,128)S(1)}, f32[32,128]{1,0:T(8,128)S(1)}, u32[]{:S(2)}, u32[]{:S(2)}) collective-permute-start(f32[32,128]{1,0:T(8,128)S(1)} %get-tuple-element.26), channel_id=1, source_target_pairs={{0,1},{1,0},{2,3},{3,2},{4,5},{5,4},{6,7},{7,6},{8,9},{9,8},{10,11... | collective-permute-start | bytes 49160 | tf_op jit(solution)/shard_map/ppermute | solution.py:370

commit v4 on v3

--- a/solution.py
+++ b/solution.py
@@ -21,7 +21,6 @@
 FIRST_INNER = 10
 FIRST_OUTER = 5
 FIRST = FIRST_OUTER * INNER + FIRST_INNER
-FIRST_LAST = FIRST
 
 F32 = jnp.float32
 BF16 = jnp.bfloat16
@@ -31,15 +30,12 @@
 HBM = pl.BlockSpec(memory_space=pltpu.HBM)
 
 
-def transform_tables():
+def transform_table():
     times = np.arange(SPAN).reshape(INNER, -1)[np.arange(INNER) ^ FIRST_INNER]
     turns = np.outer(np.arange(L), times) % TIMES
     phase = 2.0 * np.pi / TIMES * turns
     table = np.concatenate([np.cos(phase), np.sin(phase)], axis=1) / np.sqrt(TIMES)
-    table = table.astype(np.float32)
-    high = table.astype(BF16)
-    low = (table - high.astype(np.float32)).astype(BF16)
-    return high, low
+    return table.astype(np.float32)
 
 
 def low_lanes(shape):
@@ -70,80 +66,90 @@
     return jnp.where(condition, 1.0, 0.0).astype(BF16)
 
 
-def pack_kernel(vis_ref, counts_ref, out_ref, vis, counts, packed, in_sems, out_sems, sem):
-    blocks = vis.shape[0]
-    weigh = pltpu.make_async_copy(counts_ref, counts, sem)
-    weigh.start()
-
-    def fetch(j):
-        lanes = pl.ds(j * LANES, LANES)
-        return pltpu.make_async_copy(vis_ref.at[:, :, lanes], vis.at[j], in_sems.at[j])
-
-    def store(j):
-        two = pl.ds(2 * j, 2)
-        return pltpu.make_async_copy(packed.at[two], out_ref.at[two], out_sems.at[j])
-
-    for j in range(blocks):
-        fetch(j).start()
-    weigh.wait()
-    low = low_lanes(vis.shape[2:])
-    for j in range(blocks):
-        fetch(j).wait()
-        scale = counts[j : j + 1, :].astype(F32) * (1.0 / 256.0)
-        re = vis[j, 0] * scale
-        im = vis[j, 1] * scale
-        packed[2 * j] = jnp.where(low, re, pltpu.roll(im, HALF, 1))
-        packed[2 * j + 1] = jnp.where(low, pltpu.roll(re, HALF, 1), im)
-        store(j).start()
-    for j in range(blocks):
-        store(j).wait()
-
-
-def tables_kernel(
-    outer_ref, high_hbm, low_hbm, order_hbm, high_ref, low_ref, pick_ref, turn_ref, order, sems
-):
+def pack_kernel(vis_ref, counts_ref, out_ref, vis, counts, packed, in_sems, out_sems):
     copies = [
-        pltpu.make_async_copy(order_hbm, order.at[pl.ds(0, L // LANES)], sems.at[0]),
-        pltpu.make_async_copy(high_hbm, high_ref, sems.at[1]),
-        pltpu.make_async_copy(low_hbm, low_ref, sems.at[2]),
+        pltpu.make_async_copy(vis_ref, vis, in_sems.at[0]),
+        pltpu.make_async_copy(counts_ref, counts, in_sems.at[1]),
     ]
     for copy in copies:
         copy.start()
+    for copy in copies:
+        copy.wait()
+
+    def store(i):
+        part = pl.ds(i * INNER // 2, INNER // 2)
+        return pltpu.make_async_copy(packed.at[part], out_ref.at[part], out_sems.at[i])
+
+    blocks = vis.shape[2] // LANES
+    low = low_lanes((vis.shape[1], LANES))
+    for j in range(blocks):
+        lanes = slice(j * LANES, (j + 1) * LANES)
+        scale = counts[j : j + 1, :].astype(F32) * (1.0 / 256.0)
+        re = vis[0, :, lanes] * scale
+        im = vis[1, :, lanes] * scale
+        packed[2 * j] = jnp.where(low, re, pltpu.roll(im, HALF, 1))
+        packed[2 * j + 1] = jnp.where(low, pltpu.roll(re, HALF, 1), im)
+        if j % (blocks // 2) == blocks // 2 - 1:
+            store(2 * j // blocks).start()
+    for i in range(2):
+        store(i).wait()
+
+
+def tables_kernel(
+    outer_ref, table_hbm, order_hbm, high_ref, low_ref, table, high, low, pick, order, sems
+):
+    order_copy = pltpu.make_async_copy(order_hbm, order.at[pl.ds(0, L // LANES)], sems.at[0])
+    order_copy.start()
+
+    def fetch(i):
+        rows = pl.ds(i * LANES, LANES)
+        return pltpu.make_async_copy(table_hbm.at[rows], table.at[rows], sems.at[i + 1])
+
+    for i in range(L // LANES):
+        fetch(i).start()
     eighths = lax.broadcasted_iota(I32, (8, LANES), 0) * outer_ref[0] % 8
     angle = eighths.astype(F32) * (2.0 * np.pi / 8)
-    turn_ref[0] = jnp.cos(angle)
-    turn_ref[1] = jnp.sin(angle)
-    copies[0].wait()
+    along = jnp.cos(angle)[None, :, :1]
+    across = jnp.sin(angle)[None, :, :1]
+
+    order_copy.wait()
     columns = lane_xor(order[...], SLOTS * FIRST % LANES).T
     modes = lax.broadcasted_iota(I32, (LANES, L), 1)
     for i in range(L // LANES):
         block = i ^ SLOTS * FIRST // LANES
-        pick_ref[i * LANES : (i + 1) * LANES, :] = ones_where(
-            modes == columns[:, block : block + 1]
-        )
-    copies[1].wait()
-    copies[2].wait()
-
-
-def transform_kernel(
-    x_ref, high_ref, low_ref, pick_ref, turn_ref, out_ref, token_ref, slots_ref, sem
-):
+        pick[i * LANES : (i + 1) * LANES, :] = ones_where(modes == columns[:, block : block + 1])
+
+    for i in range(L // LANES):
+        fetch(i).wait()
+        rows = slice(i * LANES, (i + 1) * LANES)
+        cosine = table[rows, :SPAN].reshape(LANES // 8, 8, SPAN)
+        sine = table[rows, SPAN:].reshape(LANES // 8, 8, SPAN)
+        turned = [cosine * along - sine * across, sine * along + cosine * across]
+        turned = jnp.concatenate([part.reshape(LANES, SPAN) for part in turned], axis=1)
+        high[rows, :], low[rows, :] = split(turned)
+    for i in range(L // LANES):
+        rows = slice(i * LANES, (i + 1) * LANES)
+        for part, out_ref in ((high, high_ref), (low, low_ref)):
+            picked = jnp.dot(pick[rows, :], part[...], preferred_element_type=F32)
+            out_ref[rows, :] = picked.astype(BF16)
+
+
+def transform_kernel(x_ref, high_ref, low_ref, out_ref, token_ref, slots_ref, sems):
+    token_ref[...] = jnp.zeros_like(token_ref)
     x = x_ref[...]
     high, low = split(jnp.concatenate([x, quarter_turn(x)], axis=0))
-    wide = jnp.dot(
-        high_ref[...], jnp.concatenate([high, low], axis=1), preferred_element_type=F32
-    )
-    modes = wide[:, :LANES] + wide[:, LANES:]
-    modes = modes + jnp.dot(low_ref[...], high, preferred_element_type=F32)
-    turned = quarter_turn(modes).reshape(L // 8, 8, LANES)
-    modes = modes.reshape(L // 8, 8, LANES) * turn_ref[0][None] + turned * turn_ref[1][None]
-    parts = jnp.concatenate(split(modes.reshape(L, LANES)), axis=1)
-    slots = jnp.dot(pick_ref[...], parts, preferred_element_type=F32)
-    slots_ref[...] = slots[:, :LANES] + slots[:, LANES:]
-    token_ref[...] = jnp.zeros_like(token_ref)
-    store = pltpu.make_async_copy(slots_ref, out_ref, sem)
-    store.start()
-    store.wait()
+    both = jnp.concatenate([high, low], axis=1)
+    copies = []
+    for i in range(2):
+        rows = slice(i * L // 2, (i + 1) * L // 2)
+        wide = jnp.dot(high_ref[rows, :], both, preferred_element_type=F32)
+        slots = jnp.dot(low_ref[rows, :], high, preferred_element_type=F32)
+        slots_ref[rows, :] = slots + wide[:, :LANES] + wide[:, LANES:]
+        half = pl.ds(i * L // 2, L // 2)
+        copies.append(pltpu.make_async_copy(slots_ref.at[half], out_ref.at[half], sems.at[i]))
+        copies[i].start()
+    for copy in copies:
+        copy.wait()
 
 
 def held_kernel(
@@ -177,7 +183,7 @@
     rows_copy.wait()
     counts = jnp.broadcast_to(rows[...], (ROWCAP, OWNERS)).astype(F32).astype(BF16)
     other = lax.broadcasted_iota(I32, (OWNERS, OWNERS), 0)
-    owner = lax.broadcasted_iota(I32, (OWNERS, OWNERS), 1) ^ FIRST_LAST
+    owner = lax.broadcasted_iota(I32, (OWNERS, OWNERS), 1) ^ FIRST
     starts = jnp.dot(counts, ones_where(other < owner), preferred_element_type=F32)
     counts = jnp.dot(counts, ones_where(other == owner), preferred_element_type=F32)
     counts = counts.astype(I32)
@@ -254,7 +260,8 @@
 
 
 def finish_kernel(parts_ref, out_ref):
-    out_ref[...] = lane_xor(parts_ref[...].T, FIRST_LAST)
+    tiles = [parts_ref[(i ^ FIRST // 8) * 8 : (i ^ FIRST // 8) * 8 + 8, :] for i in range(OWNERS // 8)]
+    out_ref[...] = lane_xor(jnp.concatenate(tiles, axis=0).T, FIRST % 8)
 
 
 def exchange(array, first, size):
@@ -290,7 +297,7 @@
     core = lax.axis_index("bl")
     share = vis.shape[1]
     blocks = vis.shape[2] // LANES
-    high, low = transform_tables()
+    table = transform_table()
     dma = pltpu.SemaphoreType.DMA
 
     packed = call(
@@ -298,37 +305,38 @@
         pltpu.HBM((INNER, share, LANES), F32),
         [HBM, HBM],
         [
-            pltpu.VMEM((blocks, 2, share, LANES), F32),
+            pltpu.VMEM(vis.shape, F32),
             pltpu.VMEM((blocks, LANES), I32),
             pltpu.VMEM((INNER, share, LANES), F32),
-            dma((blocks,)),
-            dma((blocks,)),
-            dma(()),
+            dma((2,)),
+            dma((2,)),
         ],
     )(in_hbm(vis), in_hbm(counts.reshape(blocks, LANES)))
     gathered = exchange(packed, FIRST_INNER, INNER)
 
     tables = call(
         tables_kernel,
-        (
-            pltpu.VMEM(high.shape, BF16),
-            pltpu.VMEM(low.shape, BF16),
+        (pltpu.VMEM(table.shape, BF16), pltpu.VMEM(table.shape, BF16)),
+        [SMEM, HBM, HBM],
+        [
+            pltpu.VMEM(table.shape, F32),
+            pltpu.VMEM(table.shape, BF16),
+            pltpu.VMEM(table.shape, BF16),
             pltpu.VMEM((L, L), BF16),
-            pltpu.VMEM((2, 8, LANES), F32),
-        ),
-        [SMEM, HBM, HBM, HBM],
-        [pltpu.VMEM((8, LANES), I32), dma((3,))],
+            pltpu.VMEM((8, LANES), I32),
+            dma((L // LANES + 1,)),
+        ],
+        scoped=16,
     )(
         (place // INNER).astype(I32).reshape(1),
-        in_hbm(jnp.asarray(high)),
-        in_hbm(jnp.asarray(low)),
+        in_hbm(jnp.asarray(table)),
         in_hbm(m_order.reshape(L // LANES, LANES)),
     )
     modes, token = call(
         transform_kernel,
         (pltpu.HBM((L, LANES), F32), pltpu.VMEM((8, LANES), F32)),
-        [VMEM] * 5,
-        [pltpu.VMEM((L, LANES), F32), dma(())],
+        [VMEM] * 3,
+        [pltpu.VMEM((L, LANES), F32), dma((2,))],
     )(gathered.reshape(SPAN, LANES), *map(in_vmem, tables))
     sums = exchange(modes.reshape(OWNERS, SLOTS, LANES), FIRST, OWNERS)
 
@@ -368,7 +376,7 @@
         beam,
     )
     picked = own + lax.ppermute(other, "bl", [(0, 1), (1, 0)])
-    received = exchange(picked.T, FIRST_LAST, OWNERS)
+    received = exchange(picked.T, FIRST, OWNERS)
     out = call(finish_kernel, jax.ShapeDtypeStruct((4 * ROWCAP, OWNERS), F32), [VMEM])(received)
     return out.reshape(2, 2, ROWCAP, OWNERS).transpose(0, 3, 1, 2)
 

time: 63.4 us -> 62.1 us (0.979)
  waiting for transfers between devices: 7.01 us -> 5.65 us
    all_to_all x2, waiting for transfers between devices: 6.17 us -> 4.81 us  [exchange(): lax.all_to_all(array, 'ma', 0, 0, axis_index_groups=groups, tiled=True)]
    pallas_call x1, Pallas kernels: 1.58 us -> 2.94 us  [body(): call(tables_kernel, (pltpu.VMEM(table.shape, BF16), pltpu.VMEM(table.shap...]
  transfers between devices with their start and end apart: 3 -> 3, of which waited for: 3 -> 3; matrix products, arithmetic and copies ran while one was open for 0% -> 0% of each run, Pallas kernels for 6% -> 8%
where the time goes in v4:
time: 62.1 us; the launch traced here: 61.8 us
  starting transfers between devices  27.6 us (44%)
  blocking collectives  16.1 us (26%)
  Pallas kernels  12.2 us (20%)
  waiting for transfers between devices  5.65 us (9%)
    all_to_all x2, starting transfers between devices, exchange(): lax.all_to_all(array, 'ma', 0, 0, axis_index_groups=groups, tiled=True)  25.3 us
    all_to_all x1, blocking collectives, exchange(): lax.all_to_all(array, 'ma', 0, 0, axis_index_groups=groups, tiled=True)  16.1 us
    all_to_all x2, waiting for transfers between devices, exchange(): lax.all_to_all(array, 'ma', 0, 0, axis_index_groups=groups, tiled=True)  4.81 us
    pallas_call x1, Pallas kernels, body(): call(project_kernel, (half, half), [SMEM] + [VMEM] * 4 + [HBM], [pltpu.VM...  3.43 us
    pallas_call x1, Pallas kernels, body(): call(tables_kernel, (pltpu.VMEM(table.shape, BF16), pltpu.VMEM(table.shap...  2.94 us
    ppermute x1, starting transfers between devices, body(): picked = own + lax.ppermute(other, 'bl', [(0, 1), (1, 0)])  2.29 us
    pallas_call x1, Pallas kernels, body(): call(held_kernel, (pltpu.VMEM((HELD, *beam.shape[1:]), BF16), pltpu.VMEM(...  1.94 us
    pallas_call x1, Pallas kernels, body(): call(pack_kernel, pltpu.HBM((INNER, share, LANES), F32), [HBM, HBM], [plt...  1.78 us
  transfers between devices with their start and end apart: 3, of which 3 were waited for; matrix products, arithmetic and copies ran while one was open for 0% of the time, Pallas kernels for 8%

profile of v4, /device:TPU:1, one launch (start us, length us, event | category | flops | bytes accessed | tf_op | source)
XLA Modules:
  0.0 61.8 jit_solution(10931338925925529617)
XLA Ops:
  0.0 1.8 %shard_map.64 = f32[16,32,128]{2,1,0:T(8,128)} custom-call(f32[2,32,1024]{2,1,0:T(8,128)} %vis_ref.1, s32[8,128]{1,0:T(8,128)} %bitcast.25), custom_call_target="tpu_custom_call" | custom-call | tf_op jit(solution)/shard_map/pallas_call | solution.py:303
  1.8 9.6 %all-to-all-start = ((f32[16,32,128]{2,1,0:T(8,128)}), f32[16,32,128]{2,1,0:T(8,128)S(1)}, u32[]{:S(2)}, u32[]{:S(2)}) async-start(f32[16,32,128]{2,1,0:T(8,128)} %shard_map.64), calls=%async_computation | async-start | bytes 524288 | tf_op jit(solution)/shard_map/all_to_all | solution.py:271
  11.4 2.9 %shard_map.65 = (bf16[512,1024]{1,0:T(8,128)(2,1)S(1)}, bf16[512,1024]{1,0:T(8,128)(2,1)S(1)}) custom-call(s32[1]{0:T(128)} %bitcast.3.outer_ref, f32[512,1024]{1,0:T(8,128)} %constant.26.clone.table_hbm, s32[4,128]{1,0:T(4,128)} %bitcast.24), custom_call_target="tpu_custom_call" | custom-call | tf_op jit(solution)/shard_map/pallas_call | solution.py:317
  14.3 1.3 %all-to-all-done = f32[16,32,128]{2,1,0:T(8,128)S(1)} async-done(((f32[16,32,128]{2,1,0:T(8,128)}), f32[16,32,128]{2,1,0:T(8,128)S(1)}, u32[]{:S(2)}, u32[]{:S(2)}) %all-to-all-start) | async-done | bytes 262176 | tf_op jit(solution)/shard_map/all_to_all | solution.py:271
  15.6 1.4 %shard_map.66 = (f32[512,128]{1,0:T(8,128)}, f32[8,128]{1,0:T(8,128)S(1)}) custom-call(f32[512,128]{1,0:T(8,128)S(1)} %bitcast.18, bf16[512,1024]{1,0:T(8,128)(2,1)S(1)} %get-tuple-element.14.high_ref, bf16[512,1024]{1,0:T(8,128)(2,1)S(1)} %get-tuple-element.15.low_ref), custom_call_target="tpu_custom_call" | custom-call | tf_op jit(solution)/shard_map/pallas_call | solution.py:335
  17.0 15.7 %all-to-all-start.1 = ((f32[128,4,128]{2,1,0:T(4,128)}), f32[128,4,128]{2,1,0:T(4,128)S(1)}, u32[]{:S(2)}, u32[]{:S(2)}) async-start(f32[128,4,128]{2,1,0:T(4,128)} %bitcast.23), calls=%async_computation.1 | async-start | bytes 524288 | tf_op jit(solution)/shard_map/all_to_all | solution.py:271
  32.7 1.9 %shard_map.67 = (bf16[6,512,512]{2,1,0:T(8,128)(2,1)S(1)}, s32[8,128]{1,0:T(8,128)S(1)}, f32[8,512]{1,0:T(8,128)S(1)}) custom-call(s32[1]{0:T(128)} %bitcast.7.place_ref, f32[8,128]{1,0:T(8,128)S(1)} %get-tuple-element.17.token_ref, s32[512]{0:T(512)} %order_hbm.1, s32[1,128]{1,0:T(1,128)} %bitcast.26, bf16[16,512,512]{2,1,0:T(8,128)(2,1)} %bitcast.21), custom_call_target="tpu_custom_call" | custom-call | tf_op jit(solution)/shard_map/pallas_call | solution.py:344
  34.6 3.6 %all-to-all-done.1 = f32[128,4,128]{2,1,0:T(4,128)S(1)} async-done(((f32[128,4,128]{2,1,0:T(4,128)}), f32[128,4,128]{2,1,0:T(4,128)S(1)}, u32[]{:S(2)}, u32[]{:S(2)}) %all-to-all-start.1) | async-done | bytes 262176 | tf_op jit(solution)/shard_map/all_to_all | solution.py:271
  38.2 3.4 %shard_map.68 = (f32[32,128]{1,0:T(8,128)S(1)}, f32[32,128]{1,0:T(8,128)S(1)}) custom-call(s32[1]{0:T(128)} %bitcast.core_ref, f32[512,128]{1,0:T(8,128)S(1)} %bitcast.19, bf16[6,512,512]{2,1,0:T(8,128)(2,1)S(1)} %get-tuple-element.18.held_ref, s32[8,128]{1,0:T(8,128)S(1)} %get-tuple-element.19.wanted_ref, f32[8,512]{1,0:T(8,128)S(1)} %get-tuple-element.20.keep_ref, ...), custom_call_target="tpu_custom_call" | custom-call | tf_op jit(solution)/shard_map/pallas_call | solution.py:362
  41.6 2.3 %collective-permute-start = (f32[32,128]{1,0:T(8,128)S(1)}, f32[32,128]{1,0:T(8,128)S(1)}, u32[]{:S(2)}, u32[]{:S(2)}) collective-permute-start(f32[32,128]{1,0:T(8,128)S(1)} %get-tuple-element.22), channel_id=1, source_target_pairs={{0,1},{1,0},{2,3},{3,2},{4,5},{5,4},{6,7},{7,6},{8,9},{9,8},{10,11... | collective-permute-start | bytes 49160 | tf_op jit(solution)/shard_map/ppermute | solution.py:378
  43.9 0.8 %collective-permute-done = f32[32,128]{1,0:T(8,128)S(1)} collective-permute-done((f32[32,128]{1,0:T(8,128)S(1)}, f32[32,128]{1,0:T(8,128)S(1)}, u32[]{:S(2)}, u32[]{:S(2)}) %collective-permute-start) | collective-permute-done | bytes 16416 | tf_op jit(solution)/shard_map/ppermute | solution.py:378
  44.8 0.1 copy.9
  44.9 16.1 %all_to_all.21 = f32[128,1,32]{2,1,0:T(1,128)S(1)} all-to-all(f32[128,1,32]{2,1,0:T(1,128)S(1)} %copy.9), channel_id=1, replica_groups={{180,182,176,178,188,190,184,186,164,166,160,162,172,174,168,170,148,15..., dimensions={0} | all-to-all | bytes 32768 | tf_op jit(solution)/shard_map/all_to_all | solution.py:271
  61.0 0.8 %shard_map.69 = f32[32,128]{1,0:T(8,128)} custom-call(f32[128,32]{1,0:T(8,128)S(1)} %bitcast.20), custom_call_target="tpu_custom_call" | custom-call | tf_op jit(solution)/shard_map/pallas_call | solution.py:380
  (1 shorter events, 0.0 us)
Async XLA Ops:
  1.8 13.8 %all-to-all-start = ((f32[16,32,128]{2,1,0:T(8,128)}), f32[16,32,128]{2,1,0:T(8,128)S(1)}, u32[]{:S(2)}, u32[]{:S(2)}) async-start(f32[16,32,128]{2,1,0:T(8,128)} %shard_map.64), calls=%async_computation | async-start | bytes 524288 | tf_op jit(solution)/shard_map/all_to_all | solution.py:271
  17.0 21.2 %all-to-all-start.1 = ((f32[128,4,128]{2,1,0:T(4,128)}), f32[128,4,128]{2,1,0:T(4,128)S(1)}, u32[]{:S(2)}, u32[]{:S(2)}) async-start(f32[128,4,128]{2,1,0:T(4,128)} %bitcast.23), calls=%async_computation.1 | async-start | bytes 524288 | tf_op jit(solution)/shard_map/all_to_all | solution.py:271
  41.6 3.1 %collective-permute-start = (f32[32,128]{1,0:T(8,128)S(1)}, f32[32,128]{1,0:T(8,128)S(1)}, u32[]{:S(2)}, u32[]{:S(2)}) collective-permute-start(f32[32,128]{1,0:T(8,128)S(1)} %get-tuple-element.22), channel_id=1, source_target_pairs={{0,1},{1,0},{2,3},{3,2},{4,5},{5,4},{6,7},{7,6},{8,9},{9,8},{10,11... | collective-permute-start | bytes 49160 | tf_op jit(solution)/shard_map/ppermute | solution.py:378

commit v5 on v4

--- a/solution.py
+++ b/solution.py
@@ -17,7 +17,8 @@
 LANES = 128
 HALF = 64
 PARTS = 4
-HELD = 6
+HELD = 2
+STREAM = (HELD, 10, 14, SLOTS * PARTS)
 FIRST_INNER = 10
 FIRST_OUTER = 5
 FIRST = FIRST_OUTER * INNER + FIRST_INNER
@@ -96,82 +97,55 @@
 
 
 def tables_kernel(
-    outer_ref, table_hbm, order_hbm, high_ref, low_ref, table, high, low, pick, order, sems
+    place_ref,
+    table_hbm,
+    lanes_hbm,
+    order_hbm,
+    rows_hbm,
+    beam_hbm,
+    high_ref,
+    low_ref,
+    held_ref,
+    wanted_ref,
+    keep_ref,
+    core_ref,
+    table,
+    high,
+    low,
+    pick,
+    lanes,
+    order,
+    rows,
+    sems,
 ):
-    order_copy = pltpu.make_async_copy(order_hbm, order.at[pl.ds(0, L // LANES)], sems.at[0])
+    lanes_copy = pltpu.make_async_copy(lanes_hbm, lanes.at[pl.ds(0, L // LANES)], sems.at[0])
+    order_copy = pltpu.make_async_copy(order_hbm, order, sems.at[1])
+    rows_copy = pltpu.make_async_copy(rows_hbm, rows, sems.at[2])
+    held_copy = pltpu.make_async_copy(beam_hbm.at[pl.ds(0, HELD)], held_ref, sems.at[3])
+    lanes_copy.start()
     order_copy.start()
+    rows_copy.start()
 
     def fetch(i):
-        rows = pl.ds(i * LANES, LANES)
-        return pltpu.make_async_copy(table_hbm.at[rows], table.at[rows], sems.at[i + 1])
+        part = pl.ds(i * LANES, LANES)
+        return pltpu.make_async_copy(table_hbm.at[part], table.at[part], sems.at[i + 4])
 
     for i in range(L // LANES):
         fetch(i).start()
-    eighths = lax.broadcasted_iota(I32, (8, LANES), 0) * outer_ref[0] % 8
+    held_copy.start()
+    eighths = lax.broadcasted_iota(I32, (8, LANES), 0) * (place_ref[0] // INNER) % 8
     angle = eighths.astype(F32) * (2.0 * np.pi / 8)
     along = jnp.cos(angle)[None, :, :1]
     across = jnp.sin(angle)[None, :, :1]
 
-    order_copy.wait()
-    columns = lane_xor(order[...], SLOTS * FIRST % LANES).T
+    lanes_copy.wait()
+    columns = lane_xor(lanes[...], SLOTS * FIRST % LANES).T
     modes = lax.broadcasted_iota(I32, (LANES, L), 1)
     for i in range(L // LANES):
         block = i ^ SLOTS * FIRST // LANES
         pick[i * LANES : (i + 1) * LANES, :] = ones_where(modes == columns[:, block : block + 1])
 
-    for i in range(L // LANES):
-        fetch(i).wait()
-        rows = slice(i * LANES, (i + 1) * LANES)
-        cosine = table[rows, :SPAN].reshape(LANES // 8, 8, SPAN)
-        sine = table[rows, SPAN:].reshape(LANES // 8, 8, SPAN)
-        turned = [cosine * along - sine * across, sine * along + cosine * across]
-        turned = jnp.concatenate([part.reshape(LANES, SPAN) for part in turned], axis=1)
-        high[rows, :], low[rows, :] = split(turned)
-    for i in range(L // LANES):
-        rows = slice(i * LANES, (i + 1) * LANES)
-        for part, out_ref in ((high, high_ref), (low, low_ref)):
-            picked = jnp.dot(pick[rows, :], part[...], preferred_element_type=F32)
-            out_ref[rows, :] = picked.astype(BF16)
-
-
-def transform_kernel(x_ref, high_ref, low_ref, out_ref, token_ref, slots_ref, sems):
-    token_ref[...] = jnp.zeros_like(token_ref)
-    x = x_ref[...]
-    high, low = split(jnp.concatenate([x, quarter_turn(x)], axis=0))
-    both = jnp.concatenate([high, low], axis=1)
-    copies = []
-    for i in range(2):
-        rows = slice(i * L // 2, (i + 1) * L // 2)
-        wide = jnp.dot(high_ref[rows, :], both, preferred_element_type=F32)
-        slots = jnp.dot(low_ref[rows, :], high, preferred_element_type=F32)
-        slots_ref[rows, :] = slots + wide[:, :LANES] + wide[:, LANES:]
-        half = pl.ds(i * L // 2, L // 2)
-        copies.append(pltpu.make_async_copy(slots_ref.at[half], out_ref.at[half], sems.at[i]))
-        copies[i].start()
-    for copy in copies:
-        copy.wait()
-
-
-def held_kernel(
-    place_ref,
-    token_ref,
-    order_hbm,
-    rows_hbm,
-    beam_hbm,
-    held_ref,
-    wanted_ref,
-    keep_ref,
-    order,
-    rows,
-    sems,
-):
-    rows_copy = pltpu.make_async_copy(rows_hbm, rows, sems.at[0])
-    order_copy = pltpu.make_async_copy(order_hbm, order, sems.at[1])
-    held_copy = pltpu.make_async_copy(beam_hbm.at[pl.ds(0, HELD)], held_ref, sems.at[2])
-    rows_copy.start()
-    order_copy.start()
-    held_copy.start()
-
+    core_ref[...] = jnp.broadcast_to(place_ref[1], (8, LANES))
     order_copy.wait()
     ells = lax.broadcasted_iota(I32, (1, L), 1)
     for k in range(SLOTS):
@@ -189,15 +163,38 @@
     counts = counts.astype(I32)
     within = lax.broadcasted_iota(I32, (ROWCAP, OWNERS), 0)
     wanted_ref[...] = jnp.where(within < counts, starts.astype(I32) + within, -1)
+
+    for i in range(L // LANES):
+        fetch(i).wait()
+        part = slice(i * LANES, (i + 1) * LANES)
+        cosine = table[part, :SPAN].reshape(LANES // 8, 8, SPAN)
+        sine = table[part, SPAN:].reshape(LANES // 8, 8, SPAN)
+        turned = [cosine * along - sine * across, sine * along + cosine * across]
+        turned = jnp.concatenate([half.reshape(LANES, SPAN) for half in turned], axis=1)
+        high[part, :], low[part, :] = split(turned)
+    for i in range(L // LANES):
+        part = slice(i * LANES, (i + 1) * LANES)
+        for source, out_ref in ((high, high_ref), (low, low_ref)):
+            picked = jnp.dot(pick[part, :], source[...], preferred_element_type=F32)
+            out_ref[part, :] = picked.astype(BF16)
     held_copy.wait()
 
 
+def transform_kernel(x_ref, high_ref, low_ref, out_ref):
+    x = x_ref[...]
+    high, low = split(jnp.concatenate([x, quarter_turn(x)], axis=0))
+    both = jnp.concatenate([high, low], axis=1)
+    wide = jnp.dot(high_ref[...], both, preferred_element_type=F32)
+    slots = jnp.dot(low_ref[...], high, preferred_element_type=F32)
+    out_ref[...] = slots + wide[:, :LANES] + wide[:, LANES:]
+
+
 def project_kernel(
-    core_ref,
     sums_ref,
     held_ref,
     wanted_ref,
     keep_ref,
+    core_ref,
     beam_hbm,
     own_ref,
     other_ref,
@@ -205,11 +202,12 @@
     pick,
     sems,
 ):
-    def fetch(i):
-        return pltpu.make_async_copy(beam_hbm.at[i], beam.at[i - HELD], sems.at[i - HELD])
-
-    for i in range(HELD, SLOTS * PARTS):
-        fetch(i).start()
+    copies = {}
+    for i, (begin, end) in enumerate(zip(STREAM, STREAM[1:])):
+        source = beam_hbm.at[pl.ds(begin, end - begin)]
+        target = beam.at[pl.ds(begin - HELD, end - begin)]
+        copies[begin] = pltpu.make_async_copy(source, target, sems.at[i])
+        copies[begin].start()
 
     at = lax.broadcasted_iota(I32, (L, OWNERS), 0)
     for q in range(ROWCAP):
@@ -235,7 +233,8 @@
         if i < HELD:
             block = held_ref[i]
         else:
-            fetch(i).wait()
+            if i in copies:
+                copies[i].wait()
             block = beam[i - HELD]
         part = i % PARTS * depth
         return jnp.dot(weights[:, part : part + depth], block, preferred_element_type=F32)
@@ -251,7 +250,7 @@
 
     wide = jnp.dot(alm, pick[...], preferred_element_type=F32)
     wide = wide[:8] + wide[8:]
-    first = core_ref[0] == 0
+    first = core_ref[:4] == 0
     for q in range(ROWCAP):
         block = wide[:, q * OWNERS : (q + 1) * OWNERS]
         rows_at = pl.ds(q, 4, stride=ROWCAP)
@@ -260,7 +259,8 @@
 
 
 def finish_kernel(parts_ref, out_ref):
-    tiles = [parts_ref[(i ^ FIRST // 8) * 8 : (i ^ FIRST // 8) * 8 + 8, :] for i in range(OWNERS // 8)]
+    starts = [8 * (i ^ FIRST // 8) for i in range(OWNERS // 8)]
+    tiles = [parts_ref[start : start + 8, :] for start in starts]
     out_ref[...] = lane_xor(jnp.concatenate(tiles, axis=0).T, FIRST % 8)
 
 
@@ -294,7 +294,6 @@
 
 def body(vis, counts, m_order, beam, row_counts):
     place = lax.axis_index("ma")
-    core = lax.axis_index("bl")
     share = vis.shape[1]
     blocks = vis.shape[2] // LANES
     table = transform_table()
@@ -314,63 +313,55 @@
     )(in_hbm(vis), in_hbm(counts.reshape(blocks, LANES)))
     gathered = exchange(packed, FIRST_INNER, INNER)
 
-    tables = call(
+    beam = in_hbm(beam.reshape(SLOTS * PARTS, -1, L))
+    high, low, *held = call(
         tables_kernel,
-        (pltpu.VMEM(table.shape, BF16), pltpu.VMEM(table.shape, BF16)),
-        [SMEM, HBM, HBM],
+        (
+            pltpu.VMEM(table.shape, BF16),
+            pltpu.VMEM(table.shape, BF16),
+            pltpu.VMEM((HELD, *beam.shape[1:]), BF16),
+            pltpu.VMEM((ROWCAP, OWNERS), I32),
+            pltpu.VMEM((8, L), F32),
+            pltpu.VMEM((8, LANES), I32),
+        ),
+        [SMEM] + [HBM] * 5,
         [
             pltpu.VMEM(table.shape, F32),
             pltpu.VMEM(table.shape, BF16),
             pltpu.VMEM(table.shape, BF16),
             pltpu.VMEM((L, L), BF16),
             pltpu.VMEM((8, LANES), I32),
-            dma((L // LANES + 1,)),
+            pltpu.SMEM((L,), I32),
+            pltpu.VMEM((1, OWNERS), I32),
+            dma((L // LANES + 4,)),
         ],
         scoped=16,
     )(
-        (place // INNER).astype(I32).reshape(1),
+        jnp.stack([place, lax.axis_index("bl")]).astype(I32),
         in_hbm(jnp.asarray(table)),
         in_hbm(m_order.reshape(L // LANES, LANES)),
-    )
-    modes, token = call(
-        transform_kernel,
-        (pltpu.HBM((L, LANES), F32), pltpu.VMEM((8, LANES), F32)),
-        [VMEM] * 3,
-        [pltpu.VMEM((L, LANES), F32), dma((2,))],
-    )(gathered.reshape(SPAN, LANES), *map(in_vmem, tables))
-    sums = exchange(modes.reshape(OWNERS, SLOTS, LANES), FIRST, OWNERS)
-
-    beam = in_hbm(beam.reshape(SLOTS * PARTS, -1, L))
-    held = call(
-        held_kernel,
-        (
-            pltpu.VMEM((HELD, *beam.shape[1:]), BF16),
-            pltpu.VMEM((ROWCAP, OWNERS), I32),
-            pltpu.VMEM((8, L), F32),
-        ),
-        [SMEM, VMEM, HBM, HBM, HBM],
-        [pltpu.SMEM((L,), I32), pltpu.VMEM((1, OWNERS), I32), dma((3,))],
-    )(
-        place.astype(I32).reshape(1),
-        token,
         in_hbm(m_order),
         in_hbm(row_counts.reshape(1, OWNERS)),
         beam,
     )
+    modes = call(transform_kernel, pltpu.VMEM((L, LANES), F32), [VMEM] * 3)(
+        gathered.reshape(SPAN, LANES), in_vmem(high), in_vmem(low)
+    )
+    sums = exchange(modes.reshape(OWNERS, SLOTS, LANES), FIRST, OWNERS)
+
     half = pltpu.VMEM((4 * ROWCAP, OWNERS), F32)
     streamed = SLOTS * PARTS - HELD
     own, other = call(
         project_kernel,
         (half, half),
-        [SMEM] + [VMEM] * 4 + [HBM],
+        [VMEM] * 5 + [HBM],
         [
             pltpu.VMEM((streamed, *beam.shape[1:]), BF16),
             pltpu.VMEM((L, ROWCAP * OWNERS), BF16),
-            dma((streamed,)),
+            dma((len(STREAM) - 1,)),
         ],
         scoped=24,
     )(
-        core.astype(I32).reshape(1),
         sums.reshape(OWNERS * SLOTS, LANES),
         *map(in_vmem, held),
         beam,

time: 62.1 us -> 61.4 us (0.989)
  blocking collectives: 16.1 us -> 37.2 us
  starting transfers between devices: 27.6 us -> 11.8 us
  waiting for transfers between devices: 5.65 us -> 1.3 us
  Pallas kernels: 12.2 us -> 10.6 us
    all_to_all x1 -> x2, blocking collectives: 16.1 us -> 37.2 us  [exchange(): lax.all_to_all(array, 'ma', 0, 0, axis_index_groups=groups, tiled=True)]
    all_to_all x2 -> x1, starting transfers between devices: 25.3 us -> 9.6 us  [exchange(): lax.all_to_all(array, 'ma', 0, 0, axis_index_groups=groups, tiled=True)]
    all_to_all x2 -> x1, waiting for transfers between devices: 4.81 us -> 0.46 us  [exchange(): lax.all_to_all(array, 'ma', 0, 0, axis_index_groups=groups, tiled=True)]
    pallas_call x3 -> x2, Pallas kernels: 6.76 us -> 4.37 us  [the longest x1 3.64 us: body(): call(project_kernel, (half, half), [VMEM] * 5 + [HBM], [pltpu.VMEM((strea...]
    pallas_call x1, Pallas kernels: 2.94 us -> 3.67 us  [body(): call(tables_kernel, (pltpu.VMEM(table.shape, BF16), pltpu.VMEM(table.shap...]
  transfers between devices with their start and end apart: 3 -> 2, of which waited for: 3 -> 2; matrix products, arithmetic and copies ran while one was open for 0% -> 0% of each run, Pallas kernels for 8% -> 6%
where the time goes in v5:
time: 61.4 us; the launch traced here: 61.1 us
  blocking collectives  37.2 us (61%)
  starting transfers between devices  11.8 us (19%)
  Pallas kernels  10.6 us (17%)
  waiting for transfers between devices  1.3 us (2%)
    all_to_all x2, blocking collectives, exchange(): lax.all_to_all(array, 'ma', 0, 0, axis_index_groups=groups, tiled=True)  37.2 us
    all_to_all x1, starting transfers between devices, exchange(): lax.all_to_all(array, 'ma', 0, 0, axis_index_groups=groups, tiled=True)  9.6 us
    pallas_call x1, Pallas kernels, body(): call(tables_kernel, (pltpu.VMEM(table.shape, BF16), pltpu.VMEM(table.shap...  3.67 us
    pallas_call x1, Pallas kernels, body(): call(project_kernel, (half, half), [VMEM] * 5 + [HBM], [pltpu.VMEM((strea...  3.64 us
    ppermute x1, starting transfers between devices, body(): picked = own + lax.ppermute(other, 'bl', [(0, 1), (1, 0)])  2.21 us
    pallas_call x1, Pallas kernels, body(): call(pack_kernel, pltpu.HBM((INNER, share, LANES), F32), [HBM, HBM], [plt...  1.78 us
  transfers between devices with their start and end apart: 2, of which 2 were waited for; matrix products, arithmetic and copies ran while one was open for 0% of the time, Pallas kernels for 6%

profile of v5, /device:TPU:1, one launch (start us, length us, event | category | flops | bytes accessed | tf_op | source)
XLA Modules:
  0.0 61.1 jit_solution(8917922403130418922)
XLA Ops:
  0.0 1.8 %shard_map.64 = f32[16,32,128]{2,1,0:T(8,128)} custom-call(f32[2,32,1024]{2,1,0:T(8,128)} %vis_ref.1, s32[8,128]{1,0:T(8,128)} %bitcast.24), custom_call_target="tpu_custom_call" | custom-call | tf_op jit(solution)/shard_map/pallas_call | solution.py:302
  1.8 9.6 %all-to-all-start = ((f32[16,32,128]{2,1,0:T(8,128)}), f32[16,32,128]{2,1,0:T(8,128)S(1)}, u32[]{:S(2)}, u32[]{:S(2)}) async-start(f32[16,32,128]{2,1,0:T(8,128)} %shard_map.64), calls=%async_computation | async-start | bytes 524288 | tf_op jit(solution)/shard_map/all_to_all | solution.py:271
  11.4 0.1 pad_add_fusion.place_ref
  11.5 3.7 %shard_map.65 = (bf16[512,1024]{1,0:T(8,128)(2,1)S(1)}, bf16[512,1024]{1,0:T(8,128)(2,1)S(1)}, bf16[2,512,512]{2,1,0:T(8,128)(2,1)S(1)}, s32[8,128]{1,0:T(8,128)...) custom-call(s32[2]{0:T(128)S(1)} %pad_add_fusion.place_ref, f32[512,1024]{1,0:T(8,128)} %constant.10.clone.table_hbm, ...), custom_call_target="tpu_custom_call" | custom-call | tf_op jit(solution)/shard_map/pallas_call | solution.py:317
  15.1 0.5 all-to-all-done
  15.6 0.7 %shard_map.66 = f32[512,128]{1,0:T(8,128)S(1)} custom-call(f32[512,128]{1,0:T(8,128)S(1)} %bitcast.17, bf16[512,1024]{1,0:T(8,128)(2,1)S(1)} %get-tuple-element.13.high_ref, bf16[512,1024]{1,0:T(8,128)(2,1)S(1)} %get-tuple-element.14.low_ref), custom_call_target="tpu_custom_call" | custom-call | tf_op jit(solution)/shard_map/pallas_call | solution.py:347
  16.3 21.1 %all_to_all.21 = f32[128,4,128]{2,1,0:T(4,128)S(1)} all-to-all(f32[128,4,128]{2,1,0:T(4,128)S(1)} %bitcast.19), channel_id=1, replica_groups={{180,182,176,178,188,190,184,186,164,166,160,162,172,174,168,170,148,15..., dimensions={0} | all-to-all | bytes 524288 | tf_op jit(solution)/shard_map/all_to_all | solution.py:271
  37.4 3.6 %shard_map.67 = (f32[32,128]{1,0:T(8,128)S(1)}, f32[32,128]{1,0:T(8,128)S(1)}) custom-call(f32[512,128]{1,0:T(8,128)S(1)} %bitcast.18, bf16[2,512,512]{2,1,0:T(8,128)(2,1)S(1)} %get-tuple-element.15.held_ref, s32[8,128]{1,0:T(8,128)S(1)} %get-tuple-element.16.wanted_ref, f32[8,512]{1,0:T(8,128)S(1)} %get-tuple-element.17.keep_ref, ...), custom_call_target="tpu_custom_call" | custom-call | tf_op jit(solution)/shard_map/pallas_call | solution.py:354
  41.0 2.2 %collective-permute-start = (f32[32,128]{1,0:T(8,128)S(1)}, f32[32,128]{1,0:T(8,128)S(1)}, u32[]{:S(2)}, u32[]{:S(2)}) collective-permute-start(f32[32,128]{1,0:T(8,128)S(1)} %get-tuple-element.20), channel_id=1, source_target_pairs={{0,1},{1,0},{2,3},{3,2},{4,5},{5,4},{6,7},{7,6},{8,9},{9,8},{10,11... | collective-permute-start | bytes 49160 | tf_op jit(solution)/shard_map/ppermute | solution.py:369
  43.2 0.8 %collective-permute-done = f32[32,128]{1,0:T(8,128)S(1)} collective-permute-done((f32[32,128]{1,0:T(8,128)S(1)}, f32[32,128]{1,0:T(8,128)S(1)}, u32[]{:S(2)}, u32[]{:S(2)}) %collective-permute-start) | collective-permute-done | bytes 16416 | tf_op jit(solution)/shard_map/ppermute | solution.py:369
  44.1 0.1 copy.9
  44.2 16.1 %all_to_all.22 = f32[128,1,32]{2,1,0:T(1,128)S(1)} all-to-all(f32[128,1,32]{2,1,0:T(1,128)S(1)} %copy.9), channel_id=1, replica_groups={{180,182,176,178,188,190,184,186,164,166,160,162,172,174,168,170,148,15..., dimensions={0} | all-to-all | bytes 32768 | tf_op jit(solution)/shard_map/all_to_all | solution.py:271
  60.3 0.8 %shard_map.68 = f32[32,128]{1,0:T(8,128)} custom-call(f32[128,32]{1,0:T(8,128)S(1)} %bitcast.20), custom_call_target="tpu_custom_call" | custom-call | tf_op jit(solution)/shard_map/pallas_call | solution.py:371
  (1 shorter events, 0.0 us)
Async XLA Ops:
  1.8 13.8 %all-to-all-start = ((f32[16,32,128]{2,1,0:T(8,128)}), f32[16,32,128]{2,1,0:T(8,128)S(1)}, u32[]{:S(2)}, u32[]{:S(2)}) async-start(f32[16,32,128]{2,1,0:T(8,128)} %shard_map.64), calls=%async_computation | async-start | bytes 524288 | tf_op jit(solution)/shard_map/all_to_all | solution.py:271
  41.0 3.1 %collective-permute-start = (f32[32,128]{1,0:T(8,128)S(1)}, f32[32,128]{1,0:T(8,128)S(1)}, u32[]{:S(2)}, u32[]{:S(2)}) collective-permute-start(f32[32,128]{1,0:T(8,128)S(1)} %get-tuple-element.20), channel_id=1, source_target_pairs={{0,1},{1,0},{2,3},{3,2},{4,5},{5,4},{6,7},{7,6},{8,9},{9,8},{10,11... | collective-permute-start | bytes 49160 | tf_op jit(solution)/shard_map/ppermute | solution.py:369

commit v6 on v5

--- a/solution.py
+++ b/solution.py
@@ -22,6 +22,7 @@
 FIRST_INNER = 10
 FIRST_OUTER = 5
 FIRST = FIRST_OUTER * INNER + FIRST_INNER
+FIRST_LAST = 74
 
 F32 = jnp.float32
 BF16 = jnp.bfloat16
@@ -157,7 +158,7 @@
     rows_copy.wait()
     counts = jnp.broadcast_to(rows[...], (ROWCAP, OWNERS)).astype(F32).astype(BF16)
     other = lax.broadcasted_iota(I32, (OWNERS, OWNERS), 0)
-    owner = lax.broadcasted_iota(I32, (OWNERS, OWNERS), 1) ^ FIRST
+    owner = lax.broadcasted_iota(I32, (OWNERS, OWNERS), 1) ^ FIRST_LAST
     starts = jnp.dot(counts, ones_where(other < owner), preferred_element_type=F32)
     counts = jnp.dot(counts, ones_where(other == owner), preferred_element_type=F32)
     counts = counts.astype(I32)
@@ -259,9 +260,9 @@
 
 
 def finish_kernel(parts_ref, out_ref):
-    starts = [8 * (i ^ FIRST // 8) for i in range(OWNERS // 8)]
+    starts = [8 * (i ^ FIRST_LAST // 8) for i in range(OWNERS // 8)]
     tiles = [parts_ref[start : start + 8, :] for start in starts]
-    out_ref[...] = lane_xor(jnp.concatenate(tiles, axis=0).T, FIRST % 8)
+    out_ref[...] = lane_xor(jnp.concatenate(tiles, axis=0).T, FIRST_LAST % 8)
 
 
 def exchange(array, first, size):
@@ -367,7 +368,7 @@
         beam,
     )
     picked = own + lax.ppermute(other, "bl", [(0, 1), (1, 0)])
-    received = exchange(picked.T, FIRST, OWNERS)
+    received = exchange(picked.T, FIRST_LAST, OWNERS)
     out = call(finish_kernel, jax.ShapeDtypeStruct((4 * ROWCAP, OWNERS), F32), [VMEM])(received)
     return out.reshape(2, 2, ROWCAP, OWNERS).transpose(0, 3, 1, 2)
 

time: 61.4 us -> 61.1 us (level)
  no operation moved by 1% of the time
where the time goes in v6:
time: 61.1 us; the launch traced here: 60.7 us
  blocking collectives  36.8 us (60%)
  starting transfers between devices  11.8 us (19%)
  Pallas kernels  10.6 us (17%)
  waiting for transfers between devices  1.3 us (2%)
    all_to_all x2, blocking collectives, exchange(): lax.all_to_all(array, 'ma', 0, 0, axis_index_groups=groups, tiled=True)  36.8 us
    all_to_all x1, starting transfers between devices, exchange(): lax.all_to_all(array, 'ma', 0, 0, axis_index_groups=groups, tiled=True)  9.6 us
    pallas_call x1, Pallas kernels, body(): call(tables_kernel, (pltpu.VMEM(table.shape, BF16), pltpu.VMEM(table.shap...  3.67 us
    pallas_call x1, Pallas kernels, body(): call(project_kernel, (half, half), [VMEM] * 5 + [HBM], [pltpu.VMEM((strea...  3.64 us
    ppermute x1, starting transfers between devices, body(): picked = own + lax.ppermute(other, 'bl', [(0, 1), (1, 0)])  2.21 us
    pallas_call x1, Pallas kernels, body(): call(pack_kernel, pltpu.HBM((INNER, share, LANES), F32), [HBM, HBM], [plt...  1.78 us
  transfers between devices with their start and end apart: 2, of which 2 were waited for; matrix products, arithmetic and copies ran while one was open for 0% of the time, Pallas kernels for 6%

profile of v6, /device:TPU:1, one launch (start us, length us, event | category | flops | bytes accessed | tf_op | source)
XLA Modules:
  0.0 60.7 jit_solution(9614235962088699620)
XLA Ops:
  0.0 1.8 %shard_map.64 = f32[16,32,128]{2,1,0:T(8,128)} custom-call(f32[2,32,1024]{2,1,0:T(8,128)} %vis_ref.1, s32[8,128]{1,0:T(8,128)} %bitcast.24), custom_call_target="tpu_custom_call" | custom-call | tf_op jit(solution)/shard_map/pallas_call | solution.py:303
  1.8 9.6 %all-to-all-start = ((f32[16,32,128]{2,1,0:T(8,128)}), f32[16,32,128]{2,1,0:T(8,128)S(1)}, u32[]{:S(2)}, u32[]{:S(2)}) async-start(f32[16,32,128]{2,1,0:T(8,128)} %shard_map.64), calls=%async_computation | async-start | bytes 524288 | tf_op jit(solution)/shard_map/all_to_all | solution.py:272
  11.4 0.1 pad_add_fusion.place_ref
  11.5 3.7 %shard_map.65 = (bf16[512,1024]{1,0:T(8,128)(2,1)S(1)}, bf16[512,1024]{1,0:T(8,128)(2,1)S(1)}, bf16[2,512,512]{2,1,0:T(8,128)(2,1)S(1)}, s32[8,128]{1,0:T(8,128)...) custom-call(s32[2]{0:T(128)S(1)} %pad_add_fusion.place_ref, f32[512,1024]{1,0:T(8,128)} %constant.10.clone.table_hbm, ...), custom_call_target="tpu_custom_call" | custom-call | tf_op jit(solution)/shard_map/pallas_call | solution.py:318
  15.1 0.5 all-to-all-done
  15.6 0.7 %shard_map.66 = f32[512,128]{1,0:T(8,128)S(1)} custom-call(f32[512,128]{1,0:T(8,128)S(1)} %bitcast.17, bf16[512,1024]{1,0:T(8,128)(2,1)S(1)} %get-tuple-element.13.high_ref, bf16[512,1024]{1,0:T(8,128)(2,1)S(1)} %get-tuple-element.14.low_ref), custom_call_target="tpu_custom_call" | custom-call | tf_op jit(solution)/shard_map/pallas_call | solution.py:348
  16.3 21.1 %all_to_all.21 = f32[128,4,128]{2,1,0:T(4,128)S(1)} all-to-all(f32[128,4,128]{2,1,0:T(4,128)S(1)} %bitcast.19), channel_id=1, replica_groups={{180,182,176,178,188,190,184,186,164,166,160,162,172,174,168,170,148,15..., dimensions={0} | all-to-all | bytes 524288 | tf_op jit(solution)/shard_map/all_to_all | solution.py:272
  37.4 3.6 %shard_map.67 = (f32[32,128]{1,0:T(8,128)S(1)}, f32[32,128]{1,0:T(8,128)S(1)}) custom-call(f32[512,128]{1,0:T(8,128)S(1)} %bitcast.18, bf16[2,512,512]{2,1,0:T(8,128)(2,1)S(1)} %get-tuple-element.15.held_ref, s32[8,128]{1,0:T(8,128)S(1)} %get-tuple-element.16.wanted_ref, f32[8,512]{1,0:T(8,128)S(1)} %get-tuple-element.17.keep_ref, ...), custom_call_target="tpu_custom_call" | custom-call | tf_op jit(solution)/shard_map/pallas_call | solution.py:355
  41.0 2.2 %collective-permute-start = (f32[32,128]{1,0:T(8,128)S(1)}, f32[32,128]{1,0:T(8,128)S(1)}, u32[]{:S(2)}, u32[]{:S(2)}) collective-permute-start(f32[32,128]{1,0:T(8,128)S(1)} %get-tuple-element.20), channel_id=1, source_target_pairs={{0,1},{1,0},{2,3},{3,2},{4,5},{5,4},{6,7},{7,6},{8,9},{9,8},{10,11... | collective-permute-start | bytes 49160 | tf_op jit(solution)/shard_map/ppermute | solution.py:370
  43.2 0.8 %collective-permute-done = f32[32,128]{1,0:T(8,128)S(1)} collective-permute-done((f32[32,128]{1,0:T(8,128)S(1)}, f32[32,128]{1,0:T(8,128)S(1)}, u32[]{:S(2)}, u32[]{:S(2)}) %collective-permute-start) | collective-permute-done | bytes 16416 | tf_op jit(solution)/shard_map/ppermute | solution.py:370
  44.1 0.1 copy.9
  44.2 15.8 %all_to_all.22 = f32[128,1,32]{2,1,0:T(1,128)S(1)} all-to-all(f32[128,1,32]{2,1,0:T(1,128)S(1)} %copy.9), channel_id=1, replica_groups={{148,150,144,146,156,158,152,154,132,134,128,130,140,142,136,138,180,18..., dimensions={0} | all-to-all | bytes 32768 | tf_op jit(solution)/shard_map/all_to_all | solution.py:272
  60.0 0.8 %shard_map.68 = f32[32,128]{1,0:T(8,128)} custom-call(f32[128,32]{1,0:T(8,128)S(1)} %bitcast.20), custom_call_target="tpu_custom_call" | custom-call | tf_op jit(solution)/shard_map/pallas_call | solution.py:372
  (1 shorter events, 0.0 us)
Async XLA Ops:
  1.8 13.8 %all-to-all-start = ((f32[16,32,128]{2,1,0:T(8,128)}), f32[16,32,128]{2,1,0:T(8,128)S(1)}, u32[]{:S(2)}, u32[]{:S(2)}) async-start(f32[16,32,128]{2,1,0:T(8,128)} %shard_map.64), calls=%async_computation | async-start | bytes 524288 | tf_op jit(solution)/shard_map/all_to_all | solution.py:272
  41.0 3.1 %collective-permute-start = (f32[32,128]{1,0:T(8,128)S(1)}, f32[32,128]{1,0:T(8,128)S(1)}, u32[]{:S(2)}, u32[]{:S(2)}) collective-permute-start(f32[32,128]{1,0:T(8,128)S(1)} %get-tuple-element.20), channel_id=1, source_target_pairs={{0,1},{1,0},{2,3},{3,2},{4,5},{5,4},{6,7},{7,6},{8,9},{9,8},{10,11... | collective-permute-start | bytes 49160 | tf_op jit(solution)/shard_map/ppermute | solution.py:370

commit v7 on v6

--- a/solution.py
+++ b/solution.py
@@ -21,6 +21,7 @@
 STREAM = (HELD, 10, 14, SLOTS * PARTS)
 FIRST_INNER = 10
 FIRST_OUTER = 5
+FIRST_PLANE = 6
 FIRST = FIRST_OUTER * INNER + FIRST_INNER
 FIRST_LAST = 74
 
@@ -33,7 +34,7 @@
 
 
 def transform_table():
-    times = np.arange(SPAN).reshape(INNER, -1)[np.arange(INNER) ^ FIRST_INNER]
+    times = np.arange(SPAN).reshape(INNER, -1)[np.arange(INNER) ^ FIRST_PLANE]
     turns = np.outer(np.arange(L), times) % TIMES
     phase = 2.0 * np.pi / TIMES * turns
     table = np.concatenate([np.cos(phase), np.sin(phase)], axis=1) / np.sqrt(TIMES)
@@ -221,7 +222,8 @@
     low = low_lanes((8, LANES))
     with_re, with_im = [], []
     for j in range(INNER // 2):
-        tile = total[8 * j : 8 * j + 8]
+        at = 8 * (j ^ (FIRST_PLANE ^ FIRST_INNER) // 2)
+        tile = total[at : at + 8]
         rolled = pltpu.roll(tile, HALF, 1)
         re = jnp.where(low, tile, pltpu.roll(rolled, 4, 0))[:4]
         im = jnp.where(low, rolled, pltpu.roll(tile, 4, 0))[:4]
@@ -312,7 +314,7 @@
             dma((2,)),
         ],
     )(in_hbm(vis), in_hbm(counts.reshape(blocks, LANES)))
-    gathered = exchange(packed, FIRST_INNER, INNER)
+    gathered = exchange(packed, FIRST_PLANE, INNER)
 
     beam = in_hbm(beam.reshape(SLOTS * PARTS, -1, L))
     high, low, *held = call(

time: 61.1 us -> 60.8 us (level)
  blocking collectives: 36.8 us -> 35.8 us
  waiting for transfers between devices: 1.3 us -> 2.09 us
    all_to_all x1, starting transfers between devices: 9.6 us -> 8.54 us  [exchange(): lax.all_to_all(array, 'ma', 0, 0, axis_index_groups=groups, tiled=True)]
    all_to_all x2, blocking collectives: 36.8 us -> 35.8 us  [exchange(): lax.all_to_all(array, 'ma', 0, 0, axis_index_groups=groups, tiled=True)]
    ppermute x1, starting transfers between devices: 2.21 us -> 3.19 us  [body(): picked = own + lax.ppermute(other, 'bl', [(0, 1), (1, 0)])]
    all_to_all x1, waiting for transfers between devices: 0.46 us -> 1.25 us  [exchange(): lax.all_to_all(array, 'ma', 0, 0, axis_index_groups=groups, tiled=True)]
where the time goes in v7:
time: 60.8 us; the launch traced here: 60.4 us
  blocking collectives  35.8 us (59%)
  starting transfers between devices  11.7 us (19%)
  Pallas kernels  10.6 us (17%)
  waiting for transfers between devices  2.09 us (3%)
    all_to_all x2, blocking collectives, exchange(): lax.all_to_all(array, 'ma', 0, 0, axis_index_groups=groups, tiled=True)  35.8 us
    all_to_all x1, starting transfers between devices, exchange(): lax.all_to_all(array, 'ma', 0, 0, axis_index_groups=groups, tiled=True)  8.54 us
    pallas_call x1, Pallas kernels, body(): call(tables_kernel, (pltpu.VMEM(table.shape, BF16), pltpu.VMEM(table.shap...  3.67 us
    pallas_call x1, Pallas kernels, body(): call(project_kernel, (half, half), [VMEM] * 5 + [HBM], [pltpu.VMEM((strea...  3.64 us
    ppermute x1, starting transfers between devices, body(): picked = own + lax.ppermute(other, 'bl', [(0, 1), (1, 0)])  3.19 us
    pallas_call x1, Pallas kernels, body(): call(pack_kernel, pltpu.HBM((INNER, share, LANES), F32), [HBM, HBM], [plt...  1.78 us
    all_to_all x1, waiting for transfers between devices, exchange(): lax.all_to_all(array, 'ma', 0, 0, axis_index_groups=groups, tiled=True)  1.25 us
  transfers between devices with their start and end apart: 2, of which 2 were waited for; matrix products, arithmetic and copies ran while one was open for 0% of the time, Pallas kernels for 6%

profile of v7, /device:TPU:1, one launch (start us, length us, event | category | flops | bytes accessed | tf_op | source)
XLA Modules:
  0.0 60.4 jit_solution(1856284670504800415)
XLA Ops:
  0.0 1.8 %shard_map.64 = f32[16,32,128]{2,1,0:T(8,128)} custom-call(f32[2,32,1024]{2,1,0:T(8,128)} %vis_ref.1, s32[8,128]{1,0:T(8,128)} %bitcast.24), custom_call_target="tpu_custom_call" | custom-call | tf_op jit(solution)/shard_map/pallas_call | solution.py:305
  1.8 8.5 %all-to-all-start = ((f32[16,32,128]{2,1,0:T(8,128)}), f32[16,32,128]{2,1,0:T(8,128)S(1)}, u32[]{:S(2)}, u32[]{:S(2)}) async-start(f32[16,32,128]{2,1,0:T(8,128)} %shard_map.64), calls=%async_computation | async-start | bytes 524288 | tf_op jit(solution)/shard_map/all_to_all | solution.py:274
  10.3 0.1 pad_add_fusion.place_ref
  10.4 3.7 %shard_map.65 = (bf16[512,1024]{1,0:T(8,128)(2,1)S(1)}, bf16[512,1024]{1,0:T(8,128)(2,1)S(1)}, bf16[2,512,512]{2,1,0:T(8,128)(2,1)S(1)}, s32[8,128]{1,0:T(8,128)...) custom-call(s32[2]{0:T(128)S(1)} %pad_add_fusion.place_ref, f32[512,1024]{1,0:T(8,128)} %constant.10.clone.table_hbm, ...), custom_call_target="tpu_custom_call" | custom-call | tf_op jit(solution)/shard_map/pallas_call | solution.py:320
  14.1 1.2 %all-to-all-done = f32[16,32,128]{2,1,0:T(8,128)S(1)} async-done(((f32[16,32,128]{2,1,0:T(8,128)}), f32[16,32,128]{2,1,0:T(8,128)S(1)}, u32[]{:S(2)}, u32[]{:S(2)}) %all-to-all-start) | async-done | bytes 262176 | tf_op jit(solution)/shard_map/all_to_all | solution.py:274
  15.3 0.7 %shard_map.66 = f32[512,128]{1,0:T(8,128)S(1)} custom-call(f32[512,128]{1,0:T(8,128)S(1)} %bitcast.17, bf16[512,1024]{1,0:T(8,128)(2,1)S(1)} %get-tuple-element.13.high_ref, bf16[512,1024]{1,0:T(8,128)(2,1)S(1)} %get-tuple-element.14.low_ref), custom_call_target="tpu_custom_call" | custom-call | tf_op jit(solution)/shard_map/pallas_call | solution.py:350
  16.1 20.0 %all_to_all.21 = f32[128,4,128]{2,1,0:T(4,128)S(1)} all-to-all(f32[128,4,128]{2,1,0:T(4,128)S(1)} %bitcast.19), channel_id=1, replica_groups={{180,182,176,178,188,190,184,186,164,166,160,162,172,174,168,170,148,15..., dimensions={0} | all-to-all | bytes 524288 | tf_op jit(solution)/shard_map/all_to_all | solution.py:274
  36.1 3.6 %shard_map.67 = (f32[32,128]{1,0:T(8,128)S(1)}, f32[32,128]{1,0:T(8,128)S(1)}) custom-call(f32[512,128]{1,0:T(8,128)S(1)} %bitcast.18, bf16[2,512,512]{2,1,0:T(8,128)(2,1)S(1)} %get-tuple-element.15.held_ref, s32[8,128]{1,0:T(8,128)S(1)} %get-tuple-element.16.wanted_ref, f32[8,512]{1,0:T(8,128)S(1)} %get-tuple-element.17.keep_ref, ...), custom_call_target="tpu_custom_call" | custom-call | tf_op jit(solution)/shard_map/pallas_call | solution.py:357
  39.8 3.2 %collective-permute-start = (f32[32,128]{1,0:T(8,128)S(1)}, f32[32,128]{1,0:T(8,128)S(1)}, u32[]{:S(2)}, u32[]{:S(2)}) collective-permute-start(f32[32,128]{1,0:T(8,128)S(1)} %get-tuple-element.20), channel_id=1, source_target_pairs={{0,1},{1,0},{2,3},{3,2},{4,5},{5,4},{6,7},{7,6},{8,9},{9,8},{10,11... | collective-permute-start | bytes 49160 | tf_op jit(solution)/shard_map/ppermute | solution.py:372
  42.9 0.8 %collective-permute-done = f32[32,128]{1,0:T(8,128)S(1)} collective-permute-done((f32[32,128]{1,0:T(8,128)S(1)}, f32[32,128]{1,0:T(8,128)S(1)}, u32[]{:S(2)}, u32[]{:S(2)}) %collective-permute-start) | collective-permute-done | bytes 16416 | tf_op jit(solution)/shard_map/ppermute | solution.py:372
  43.8 0.1 copy.9
  43.9 15.8 %all_to_all.22 = f32[128,1,32]{2,1,0:T(1,128)S(1)} all-to-all(f32[128,1,32]{2,1,0:T(1,128)S(1)} %copy.9), channel_id=1, replica_groups={{148,150,144,146,156,158,152,154,132,134,128,130,140,142,136,138,180,18..., dimensions={0} | all-to-all | bytes 32768 | tf_op jit(solution)/shard_map/all_to_all | solution.py:274
  59.7 0.8 %shard_map.68 = f32[32,128]{1,0:T(8,128)} custom-call(f32[128,32]{1,0:T(8,128)S(1)} %bitcast.20), custom_call_target="tpu_custom_call" | custom-call | tf_op jit(solution)/shard_map/pallas_call | solution.py:374
  (1 shorter events, 0.0 us)
Async XLA Ops:
  1.8 13.5 %all-to-all-start = ((f32[16,32,128]{2,1,0:T(8,128)}), f32[16,32,128]{2,1,0:T(8,128)S(1)}, u32[]{:S(2)}, u32[]{:S(2)}) async-start(f32[16,32,128]{2,1,0:T(8,128)} %shard_map.64), calls=%async_computation | async-start | bytes 524288 | tf_op jit(solution)/shard_map/all_to_all | solution.py:274
  39.8 4.0 %collective-permute-start = (f32[32,128]{1,0:T(8,128)S(1)}, f32[32,128]{1,0:T(8,128)S(1)}, u32[]{:S(2)}, u32[]{:S(2)}) collective-permute-start(f32[32,128]{1,0:T(8,128)S(1)} %get-tuple-element.20), channel_id=1, source_target_pairs={{0,1},{1,0},{2,3},{3,2},{4,5},{5,4},{6,7},{7,6},{8,9},{9,8},{10,11... | collective-permute-start | bytes 49160 | tf_op jit(solution)/shard_map/ppermute | solution.py:372

commit v8 on v7

--- a/solution.py
+++ b/solution.py
@@ -18,7 +18,8 @@
 HALF = 64
 PARTS = 4
 HELD = 2
-STREAM = (HELD, 10, 14, SLOTS * PARTS)
+MORE = 4
+STREAM = (HELD + MORE, 10, 14, SLOTS * PARTS)
 FIRST_INNER = 10
 FIRST_OUTER = 5
 FIRST_PLANE = 6
@@ -182,13 +183,19 @@
     held_copy.wait()
 
 
-def transform_kernel(x_ref, high_ref, low_ref, out_ref):
+def transform_kernel(
+    x_ref, high_ref, low_ref, core_ref, beam_hbm, out_ref, more_ref, sem
+):
+    first = core_ref[0, 0] == 0
+    copy = pltpu.make_async_copy(beam_hbm.at[pl.ds(HELD, MORE)], more_ref, sem)
+    pl.when(first)(copy.start)
     x = x_ref[...]
     high, low = split(jnp.concatenate([x, quarter_turn(x)], axis=0))
     both = jnp.concatenate([high, low], axis=1)
     wide = jnp.dot(high_ref[...], both, preferred_element_type=F32)
     slots = jnp.dot(low_ref[...], high, preferred_element_type=F32)
     out_ref[...] = slots + wide[:, :LANES] + wide[:, LANES:]
+    pl.when(first)(copy.wait)
 
 
 def project_kernel(
@@ -197,13 +204,21 @@
     wanted_ref,
     keep_ref,
     core_ref,
+    more_ref,
     beam_hbm,
     own_ref,
     other_ref,
     beam,
     pick,
+    more,
     sems,
+    more_sem,
 ):
+    first = core_ref[0, 0] == 0
+    more_copy = pltpu.make_async_copy(
+        beam_hbm.at[pl.ds(HELD, MORE)], beam.at[pl.ds(0, MORE)], more_sem
+    )
+    pl.when(jnp.logical_not(first))(more_copy.start)
     copies = {}
     for i, (begin, end) in enumerate(zip(STREAM, STREAM[1:])):
         source = beam_hbm.at[pl.ds(begin, end - begin)]
@@ -232,19 +247,34 @@
     weights = jnp.concatenate(with_re + with_im, axis=1).astype(BF16)
     depth = weights.shape[1] // PARTS
 
-    def product(i):
-        if i < HELD:
-            block = held_ref[i]
-        else:
+    def product(i, block):
+        part = i % PARTS * depth
+        return jnp.dot(weights[:, part : part + depth], block, preferred_element_type=F32)
+
+    def add_more(blocks):
+        for k in range(2):
+            indices = [i for i in range(HELD, HELD + MORE) if i // PARTS == k]
+            more[k] = sum(product(i, blocks[i - HELD]) for i in indices)
+
+    @pl.when(first)
+    def _():
+        add_more(more_ref)
+
+    @pl.when(jnp.logical_not(first))
+    def _():
+        more_copy.wait()
+        add_more(beam)
+
+    alm = [None] * 8
+    for k in range(SLOTS):
+        both = more[k] if k < 2 else jnp.zeros((8, L), F32)
+        for i in range(k * PARTS, (k + 1) * PARTS):
             if i in copies:
                 copies[i].wait()
-            block = beam[i - HELD]
-        part = i % PARTS * depth
-        return jnp.dot(weights[:, part : part + depth], block, preferred_element_type=F32)
-
-    alm = [None] * 8
-    for k in range(SLOTS):
-        both = sum(product(k * PARTS + part) for part in range(PARTS))
+            if i < HELD:
+                both = both + product(i, held_ref[i])
+            elif i >= HELD + MORE:
+                both = both + product(i, beam[i - HELD])
         at = k // 2 * 4 + k % 2
         alm[at] = both[k : k + 1]
         alm[at + 2] = both[4 + k : 5 + k]
@@ -347,9 +377,12 @@
         in_hbm(row_counts.reshape(1, OWNERS)),
         beam,
     )
-    modes = call(transform_kernel, pltpu.VMEM((L, LANES), F32), [VMEM] * 3)(
-        gathered.reshape(SPAN, LANES), in_vmem(high), in_vmem(low)
-    )
+    modes, more = call(
+        transform_kernel,
+        (pltpu.VMEM((L, LANES), F32), pltpu.VMEM((MORE, *beam.shape[1:]), BF16)),
+        [VMEM] * 4 + [HBM],
+        [dma(())],
+    )(gathered.reshape(SPAN, LANES), in_vmem(high), in_vmem(low), in_vmem(held[-1]), beam)
     sums = exchange(modes.reshape(OWNERS, SLOTS, LANES), FIRST, OWNERS)
 
     half = pltpu.VMEM((4 * ROWCAP, OWNERS), F32)
@@ -357,16 +390,19 @@
     own, other = call(
         project_kernel,
         (half, half),
-        [VMEM] * 5 + [HBM],
+        [VMEM] * 6 + [HBM],
         [
             pltpu.VMEM((streamed, *beam.shape[1:]), BF16),
             pltpu.VMEM((L, ROWCAP * OWNERS), BF16),
+            pltpu.VMEM((2, 8, L), F32),
             dma((len(STREAM) - 1,)),
+            dma(()),
         ],
         scoped=24,
     )(
         sums.reshape(OWNERS * SLOTS, LANES),
         *map(in_vmem, held),
+        in_vmem(more),
         beam,
     )
     picked = own + lax.ppermute(other, "bl", [(0, 1), (1, 0)])

time: 60.8 us -> 61.5 us (1.012)
  starting transfers between devices: 11.7 us -> 12.4 us
    ppermute x1, starting transfers between devices: 3.19 us -> 3.91 us  [body(): picked = own + lax.ppermute(other, 'bl', [(0, 1), (1, 0)])]
where the time goes in v8:
time: 61.5 us; the launch traced here: 61.1 us
  blocking collectives  35.7 us (58%)
  starting transfers between devices  12.4 us (20%)
  Pallas kernels  10.6 us (17%)
  waiting for transfers between devices  2.08 us (3%)
    all_to_all x2, blocking collectives, exchange(): lax.all_to_all(array, 'ma', 0, 0, axis_index_groups=groups, tiled=True)  35.7 us
    all_to_all x1, starting transfers between devices, exchange(): lax.all_to_all(array, 'ma', 0, 0, axis_index_groups=groups, tiled=True)  8.54 us
    ppermute x1, starting transfers between devices, body(): picked = own + lax.ppermute(other, 'bl', [(0, 1), (1, 0)])  3.91 us
    pallas_call x1, Pallas kernels, body(): call(project_kernel, (half, half), [VMEM] * 6 + [HBM], [pltpu.VMEM((strea...  3.69 us
    pallas_call x1, Pallas kernels, body(): call(tables_kernel, (pltpu.VMEM(table.shape, BF16), pltpu.VMEM(table.shap...  3.67 us
    pallas_call x1, Pallas kernels, body(): call(pack_kernel, pltpu.HBM((INNER, share, LANES), F32), [HBM, HBM], [plt...  1.79 us
    all_to_all x1, waiting for transfers between devices, exchange(): lax.all_to_all(array, 'ma', 0, 0, axis_index_groups=groups, tiled=True)  1.25 us
  transfers between devices with their start and end apart: 2, of which 2 were waited for; matrix products, arithmetic and copies ran while one was open for 0% of the time, Pallas kernels for 6%

profile of v8, /device:TPU:1, one launch (start us, length us, event | category | flops | bytes accessed | tf_op | source)
XLA Modules:
  0.0 61.1 jit_solution(17462489232948629766)
XLA Ops:
  0.0 1.8 %shard_map.64 = f32[16,32,128]{2,1,0:T(8,128)} custom-call(f32[2,32,1024]{2,1,0:T(8,128)} %vis_ref.1, s32[8,128]{1,0:T(8,128)} %bitcast.25), custom_call_target="tpu_custom_call" | custom-call | tf_op jit(solution)/shard_map/pallas_call | solution.py:335
  1.8 8.5 %all-to-all-start = ((f32[16,32,128]{2,1,0:T(8,128)}), f32[16,32,128]{2,1,0:T(8,128)S(1)}, u32[]{:S(2)}, u32[]{:S(2)}) async-start(f32[16,32,128]{2,1,0:T(8,128)} %shard_map.64), calls=%async_computation | async-start | bytes 524288 | tf_op jit(solution)/shard_map/all_to_all | solution.py:304
  10.3 0.1 pad_add_fusion.place_ref
  10.4 3.7 %shard_map.65 = (bf16[512,1024]{1,0:T(8,128)(2,1)S(1)}, bf16[512,1024]{1,0:T(8,128)(2,1)S(1)}, bf16[2,512,512]{2,1,0:T(8,128)(2,1)S(1)}, s32[8,128]{1,0:T(8,128)...) custom-call(s32[2]{0:T(128)S(1)} %pad_add_fusion.place_ref, f32[512,1024]{1,0:T(8,128)} %constant.10.clone.table_hbm, ...), custom_call_target="tpu_custom_call" | custom-call | tf_op jit(solution)/shard_map/pallas_call | solution.py:350
  14.1 1.2 %all-to-all-done = f32[16,32,128]{2,1,0:T(8,128)S(1)} async-done(((f32[16,32,128]{2,1,0:T(8,128)}), f32[16,32,128]{2,1,0:T(8,128)S(1)}, u32[]{:S(2)}, u32[]{:S(2)}) %all-to-all-start) | async-done | bytes 262176 | tf_op jit(solution)/shard_map/all_to_all | solution.py:304
  15.3 0.7 %shard_map.66 = (f32[512,128]{1,0:T(8,128)S(1)}, bf16[4,512,512]{2,1,0:T(8,128)(2,1)S(1)}) custom-call(f32[512,128]{1,0:T(8,128)S(1)} %bitcast.17, bf16[512,1024]{1,0:T(8,128)(2,1)S(1)} %get-tuple-element.15.high_ref, bf16[512,1024]{1,0:T(8,128)(2,1)S(1)} %get-tuple-element.16.low_ref, s32[8,128]{1,0:T(8,128)S(1)} %get-tuple-element.17.core_ref, ...), custom_call_target="tpu_custom_call" | custom-call | tf_op jit(solution)/shard_map/pallas_call | solution.py:380
  16.1 19.9 %all_to_all.21 = f32[128,4,128]{2,1,0:T(4,128)S(1)} all-to-all(f32[128,4,128]{2,1,0:T(4,128)S(1)} %bitcast.20), channel_id=1, replica_groups={{180,182,176,178,188,190,184,186,164,166,160,162,172,174,168,170,148,15..., dimensions={0} | all-to-all | bytes 524288 | tf_op jit(solution)/shard_map/all_to_all | solution.py:304
  36.0 3.7 %shard_map.67 = (f32[32,128]{1,0:T(8,128)S(1)}, f32[32,128]{1,0:T(8,128)S(1)}) custom-call(f32[512,128]{1,0:T(8,128)S(1)} %bitcast.18, bf16[2,512,512]{2,1,0:T(8,128)(2,1)S(1)} %get-tuple-element.19.held_ref, s32[8,128]{1,0:T(8,128)S(1)} %get-tuple-element.20.wanted_ref, f32[8,512]{1,0:T(8,128)S(1)} %get-tuple-element.21.keep_ref, ...), custom_call_target="tpu_custom_call" | custom-call | tf_op jit(solution)/shard_map/pallas_call | solution.py:390
  39.7 3.9 %collective-permute-start = (f32[32,128]{1,0:T(8,128)S(1)}, f32[32,128]{1,0:T(8,128)S(1)}, u32[]{:S(2)}, u32[]{:S(2)}) collective-permute-start(f32[32,128]{1,0:T(8,128)S(1)} %get-tuple-element.24), channel_id=1, source_target_pairs={{0,1},{1,0},{2,3},{3,2},{4,5},{5,4},{6,7},{7,6},{8,9},{9,8},{10,11... | collective-permute-start | bytes 49160 | tf_op jit(solution)/shard_map/ppermute | solution.py:408
  43.6 0.8 %collective-permute-done = f32[32,128]{1,0:T(8,128)S(1)} collective-permute-done((f32[32,128]{1,0:T(8,128)S(1)}, f32[32,128]{1,0:T(8,128)S(1)}, u32[]{:S(2)}, u32[]{:S(2)}) %collective-permute-start) | collective-permute-done | bytes 16416 | tf_op jit(solution)/shard_map/ppermute | solution.py:408
  44.5 0.1 copy.9
  44.6 15.8 %all_to_all.22 = f32[128,1,32]{2,1,0:T(1,128)S(1)} all-to-all(f32[128,1,32]{2,1,0:T(1,128)S(1)} %copy.9), channel_id=1, replica_groups={{148,150,144,146,156,158,152,154,132,134,128,130,140,142,136,138,180,18..., dimensions={0} | all-to-all | bytes 32768 | tf_op jit(solution)/shard_map/all_to_all | solution.py:304
  60.4 0.8 %shard_map.68 = f32[32,128]{1,0:T(8,128)} custom-call(f32[128,32]{1,0:T(8,128)S(1)} %bitcast.19), custom_call_target="tpu_custom_call" | custom-call | tf_op jit(solution)/shard_map/pallas_call | solution.py:410
  (1 shorter events, 0.0 us)
Async XLA Ops:
  1.8 13.5 %all-to-all-start = ((f32[16,32,128]{2,1,0:T(8,128)}), f32[16,32,128]{2,1,0:T(8,128)S(1)}, u32[]{:S(2)}, u32[]{:S(2)}) async-start(f32[16,32,128]{2,1,0:T(8,128)} %shard_map.64), calls=%async_computation | async-start | bytes 524288 | tf_op jit(solution)/shard_map/all_to_all | solution.py:304
  39.7 4.7 %collective-permute-start = (f32[32,128]{1,0:T(8,128)S(1)}, f32[32,128]{1,0:T(8,128)S(1)}, u32[]{:S(2)}, u32[]{:S(2)}) collective-permute-start(f32[32,128]{1,0:T(8,128)S(1)} %get-tuple-element.24), channel_id=1, source_target_pairs={{0,1},{1,0},{2,3},{3,2},{4,5},{5,4},{6,7},{7,6},{8,9},{9,8},{10,11... | collective-permute-start | bytes 49160 | tf_op jit(solution)/shard_map/ppermute | solution.py:408
